TPU v7x, 128 devices: a whole 4x4x4 slice. The times are simulated.
128 devices in a mesh: leaf: 64 (over y, x, z), rhs: 2 (over core).
Axes of the slice: x: 4, y: 4, z: 4, core: 2. Of those that a mesh axis runs over, the one named last changes fastest.
Arguments:
- operand: bfloat16 [262144, 128], P('leaf', 'rhs'), may hold values from -6 to 6
- near_blocks: bfloat16 [8192, 256, 256], P(('leaf', 'rhs')), may hold values from -0.125 to 0.125
- near_row: int32 [8192], P(('leaf', 'rhs')), may hold values from 0 to 1023, as said below
- near_column: int32 [8192], P(('leaf', 'rhs')), may hold values from 0 to 1023, as said below
- row_basis: bfloat16 [1024, 256, 64], P('leaf'), may hold values from -0.375 to 0.375
- leaf_column_bases: bfloat16 [1024, 256, 64], P('leaf'), may hold values from -0.4375 to 0.4375
- lift_leaf: bfloat16 [1024, 64, 64], P('leaf'), may hold values from -0.5 to 0.5
- lift_middle: bfloat16 [512, 64, 64], P('leaf'), may hold values from -0.5 to 0.5
- spread_middle: bfloat16 [512, 64, 64], P('leaf'), may hold values from -0.75 to 0.75
- spread_leaf: bfloat16 [1024, 64, 64], P('leaf'), may hold values from -0.75 to 0.75
- couple_leaf: bfloat16 [1024, 16, 64, 64], P('leaf'), may hold values from -0.25 to 0.25
- couple_middle: bfloat16 [512, 16, 64, 64], P('leaf'), may hold values from -0.25 to 0.25
- couple_top: bfloat16 [256, 16, 64, 64], P('leaf'), may hold values from -0.25 to 0.25
- list_leaf: int32 [1024, 16], P('leaf'), may hold values from 0 to 1023, as said below
- list_middle: int32 [512, 16], P('leaf'), may hold values from 0 to 511, as said below
- list_top: int32 [256, 16], P('leaf'), may hold values from 0 to 255, as said below
- count_leaf: int32 [1024], P('leaf'), may hold values from 1 to 16, as said below
- count_middle: int32 [512], P('leaf'), may hold values from 1 to 16, as said below
- count_top: int32 [256], P('leaf'), may hold values from 1 to 16, as said below
Outputs:
- adjoint: bfloat16 [262144, 128], P('leaf', 'rhs')
Inputs may be any that keep to these rules, and one draw needn't show every extreme that they name: near_row of the blocks held by index i of leaf (rows i * 8 * 16 to (i + 1) * 8 * 16 - 1) lies in i * 16 to (i + 1) * 16 - 1; counts per leaf row are uneven. near_column of a block held by index i of leaf lies in i * 16 - 8 to (i + 1) * 16 + 7. `list_leaf`: a leaf cluster t of index i = t // 16 lists only leaf clusters of the indices i - 1, i and i + 1. `list_middle`: a middle cluster t of index i = t // 8 lists only middle clusters of the indices i - 2 to i + 2. `list_top`: a top cluster t of index i = t // 4 lists only top clusters of the indices i - 4 to i + 4. `count_leaf`: slots from count on are not used. `count_middle`: slots from count on are not used. `count_top`: slots from count on are not used.
All inputs are finite; a program needn't handle non-finite values.
Results may differ from a plain program's by a relative error of at most 0.005.
Values may be sent and summed in bfloat16 or wider, within the bound.
No kernel may reach another device: no remote copies, remote signals or barrier semaphores. Data moves between devices by JAX's collectives and lax.ppermute only.
A program may use at most 128 MiB of HBM per device.

v0:
```python
import jax
import jax.numpy as jnp
from jax import lax
from jax.sharding import PartitionSpec as P


def passed_along(block, axis, distance):
    devices = range(lax.axis_size(axis))
    route = [(i - distance, i) for i in devices if i - distance in devices]
    return lax.ppermute(block, axis, route)


def extended(cells, sides, width):
    for axis, dim in sides:
        count = lax.axis_size(axis)
        ends = count - 1
        head = lax.slice_in_dim(cells, 0, width, axis=dim)
        tail = lax.slice_in_dim(cells, cells.shape[dim] - width, cells.shape[dim], axis=dim)
        cells = jnp.concatenate(
            [
                lax.ppermute(tail, axis, [(i, (i + 1) % count) for i in range(ends)]),
                cells,
                lax.ppermute(head, axis, [((i + 1) % count, i) for i in range(ends)]),
            ],
            axis=dim,
        )
    return cells


def near_terms(blocks, row_indices, col_ids, vectors, offset, leaf_clusters, margin):
    picked = jnp.take(vectors, row_indices - offset, axis=0)
    products = jnp.einsum("bij,bir->bjr", blocks, picked, preferred_element_type=jnp.float32)
    slots = col_ids - (offset - margin)
    return jax.ops.segment_sum(products, slots, num_segments=leaf_clusters + 2 * margin)


def couple_level(coeffs, blocks, sources, entry_counts, lowest):
    picked = jnp.take(coeffs, (sources - lowest).reshape(-1), axis=0)
    picked = picked.reshape(sources.shape + coeffs.shape[1:])
    live_slot = jnp.arange(sources.shape[1])[None, :] < entry_counts[:, None]
    picked = jnp.where(live_slot[:, :, None, None], picked, jnp.zeros((), jnp.bfloat16))
    return jnp.einsum("tjkm,tjkr->tmr", blocks, picked, preferred_element_type=jnp.float32)


def lift(transfer, child):
    pairs = transfer.shape[0] // 2
    skeleton = transfer.shape[1]
    shaped = transfer.reshape(pairs, 2, skeleton, skeleton)
    kids = child.reshape(pairs, 2, skeleton, child.shape[2])
    return jnp.einsum("pckm,pckr->pmr", shaped, kids, preferred_element_type=jnp.float32).astype(
        jnp.bfloat16
    )


def descend(transfer, parent):
    pairs = transfer.shape[0] // 2
    skeleton = transfer.shape[1]
    shaped = transfer.reshape(pairs, 2, skeleton, skeleton).astype(jnp.float32)
    spread = jnp.einsum("pcmn,pnr->pcmr", shaped, parent, precision=lax.Precision.HIGHEST)
    return spread.reshape(2 * pairs, skeleton, parent.shape[2])


def middle_window(coeffs):
    pieces = []
    for step in range(2, -3, -1):
        if step == 0:
            pieces.append(coeffs)
        else:
            pieces.append(passed_along(coeffs, "leaf", step))
    return jnp.concatenate(pieces, axis=0)


def top_window(coeffs):
    pieces = []
    for step in range(4, -5, -1):
        if step == 0:
            pieces.append(coeffs)
        else:
            pieces.append(passed_along(coeffs, "leaf", step))
    return jnp.concatenate(pieces, axis=0)


def shards(
    operand,
    near_blocks,
    near_row,
    near_column,
    row_basis,
    leaf_column_bases,
    lift_leaf,
    lift_middle,
    spread_middle,
    spread_leaf,
    couple_leaf,
    couple_middle,
    couple_top,
    list_leaf,
    list_middle,
    list_top,
    count_leaf,
    count_middle,
    count_top,
):
    leaf_clusters = row_basis.shape[0]
    leaf_rows = row_basis.shape[1]
    columns = operand.shape[1]
    margin = leaf_clusters // 2
    device = lax.axis_index("leaf")
    offset = device * leaf_clusters
    local_rhs = operand.reshape(leaf_clusters, leaf_rows, columns)
    blocks, row_indices, col_ids = (
        lax.all_gather(near_blocks, "rhs", axis=0, tiled=True),
        lax.all_gather(near_row, "rhs", axis=0, tiled=True),
        lax.all_gather(near_column, "rhs", axis=0, tiled=True),
    )
    buffer = near_terms(blocks, row_indices, col_ids, local_rhs, offset, leaf_clusters, margin)
    low_pad = buffer[:margin]
    middle = buffer[margin : margin + leaf_clusters]
    high_pad = buffer[margin + leaf_clusters :]
    from_left = passed_along(high_pad, "leaf", 1)
    from_right = passed_along(low_pad.astype(jnp.bfloat16), "leaf", -1).astype(low_pad.dtype)
    nearfield_sum = middle + jnp.concatenate([from_left, from_right], axis=0)
    coeff_leaf = jnp.einsum(
        "lik,lir->lkr", row_basis, local_rhs, preferred_element_type=jnp.float32
    ).astype(jnp.bfloat16)
    coeff_middle = lift(lift_leaf, coeff_leaf)
    coeff_top = lift(lift_middle, coeff_middle)
    window = extended(coeff_leaf, (("leaf", 0),), leaf_clusters)
    middle_count = coeff_middle.shape[0]
    top_count = coeff_top.shape[0]
    middle_source = middle_window(coeff_middle)
    top_source = top_window(coeff_top)
    top_lowest = (device - 4) * top_count
    middle_lowest = (device - 2) * middle_count
    down_top = couple_level(top_source, couple_top, list_top, count_top, top_lowest)
    downward_middle = couple_level(
        middle_source, couple_middle, list_middle, count_middle, middle_lowest
    ) + descend(spread_middle, down_top)
    downward_leaf = couple_level(
        window, couple_leaf, list_leaf, count_leaf, offset - leaf_clusters
    ) + descend(spread_leaf, downward_middle)
    farfield_sum = jnp.einsum(
        "qdu,qup->qdp",
        leaf_column_bases.astype(jnp.float32),
        downward_leaf,
        precision=lax.Precision.HIGHEST,
    )
    return (
        (nearfield_sum + farfield_sum)
        .astype(jnp.bfloat16)
        .reshape(leaf_clusters * leaf_rows, columns)
    )


def solution(mesh):
    return jax.shard_map(
        shards,
        mesh=mesh,
        in_specs=(
            P("leaf", "rhs"),
            P(("leaf", "rhs"), None, None),
            P(("leaf", "rhs")),
            P(("leaf", "rhs")),
            P("leaf", None, None),
            P("leaf", None, None),
            P("leaf", None, None),
            P("leaf", None, None),
            P("leaf", None, None),
            P("leaf", None, None),
            P("leaf", None, None, None),
            P("leaf", None, None, None),
            P("leaf", None, None, None),
            P("leaf", None),
            P("leaf", None),
            P("leaf", None),
            P("leaf"),
            P("leaf"),
            P("leaf"),
        ),
        out_specs=P("leaf", "rhs"),
        check_vma=False,
    )
```

profile of v0, /device:TPU:16, one launch (start us, length us, event | category | flops | bytes accessed | tf_op | source)
XLA Modules:
  0.0 170.4 jit_solution(18178437029482625671)
XLA Ops:
  11.2 3.4 %collective-permute-start.8 = (bf16[4,64,64]{1,2,0:T(8,128)(2,1)S(1)}, bf16[4,64,64]{1,2,0:T(8,128)(2,1)S(1)}, u32[]{:S(2)}, u32[]{:S(2)}) collective-permute-start(bf16[4,64,64]{1,2,0:T(8,128)(2,1)S(1)} %fusion.36), channel_id=1, source_target_pairs={{0,8},{2,10},{4,12},{6,14},{8,16},{10,18},{12,20},{14,22},{16,24},... | collective-permute-start | bytes 98312 | tf_op jit(solution)/shard_map/ppermute | solution.py:10
  14.6 5.9 %collective-permute-start.9 = (bf16[4,64,64]{1,2,0:T(8,128)(2,1)S(1)}, bf16[4,64,64]{1,2,0:T(8,128)(2,1)}, u32[]{:S(2)}, u32[]{:S(2)}) collective-permute-start(bf16[4,64,64]{1,2,0:T(8,128)(2,1)S(1)} %fusion.36), channel_id=1, source_target_pairs={{0,6},{2,8},{4,10},{6,12},{8,14},{10,16},{12,18},{14,20},{16,22},{... | collective-permute-start | bytes 98312 | tf_op jit(solution)/shard_map/ppermute | solution.py:10
  20.5 2.8 %collective-permute-start.10 = (bf16[4,64,64]{1,2,0:T(8,128)(2,1)S(1)}, bf16[4,64,64]{1,2,0:T(8,128)(2,1)}, u32[]{:S(2)}, u32[]{:S(2)}) collective-permute-start(bf16[4,64,64]{1,2,0:T(8,128)(2,1)S(1)} %fusion.36), channel_id=1, source_target_pairs={{0,4},{2,6},{4,8},{6,10},{8,12},{10,14},{12,16},{14,18},{16,20},{1... | collective-permute-start | bytes 98312 | tf_op jit(solution)/shard_map/ppermute | solution.py:10
  23.3 3.2 %collective-permute-start.11 = (bf16[4,64,64]{1,2,0:T(8,128)(2,1)S(1)}, bf16[4,64,64]{1,2,0:T(8,128)(2,1)}, u32[]{:S(2)}, u32[]{:S(2)}) collective-permute-start(bf16[4,64,64]{1,2,0:T(8,128)(2,1)S(1)} %fusion.36), channel_id=1, source_target_pairs={{0,2},{2,4},{4,6},{6,8},{8,10},{10,12},{12,14},{14,16},{16,18},{18... | collective-permute-start | bytes 98312 | tf_op jit(solution)/shard_map/ppermute | solution.py:10
  26.5 6.8 %collective-permute-start.12 = (bf16[4,64,64]{1,2,0:T(8,128)(2,1)S(1)}, bf16[4,64,64]{1,2,0:T(8,128)(2,1)}, u32[]{:S(2)}, u32[]{:S(2)}) collective-permute-start(bf16[4,64,64]{1,2,0:T(8,128)(2,1)S(1)} %fusion.36), channel_id=1, source_target_pairs={{2,0},{4,2},{6,4},{8,6},{10,8},{12,10},{14,12},{16,14},{18,16},{20... | collective-permute-start | bytes 98312 | tf_op jit(solution)/shard_map/ppermute | solution.py:10
  34.7 1.3 compare_and_fusion
  39.6 1.8 %all-reduce.2 = (s32[128]{0:T(128)S(1)}, s32[128]{0:T(128)S(1)}) all-reduce(s32[128]{0:T(128)S(1)} %dynamic-update-slice, s32[128]{0:T(128)S(1)} %dynamic-update-slice.1), channel_id=1, replica_groups=mesh['leaf'=64,'rhs'=2] {'rhs'}, use_global_device_ids=true, to_apply=%add | all-reduce | flops 256 | bytes 2048
  43.8 1.3 iota_compare_fusion.1
  45.1 2.8 %gather_fusion = bf16[128,256,64]{1,2,0:T(8,128)(2,1)} fusion(bf16[16,256,64]{1,2,0:T(8,128)(2,1)S(1)} %bitcast.92, s32[1024]{0:T(1024)S(1)} %pad_clamp_fusion.3), kind=kCustom, calls=%fused_computation | custom fusion | bytes 8389120 | tf_op jit(solution)/shard_map/jit(_take)/gather | solution.py:31
  48.6 3.4 %collective-permute-start.13 = (bf16[4,64,64]{1,2,0:T(8,128)(2,1)S(1)}, bf16[4,64,64]{1,2,0:T(8,128)(2,1)S(1)}, u32[]{:S(2)}, u32[]{:S(2)}) collective-permute-start(bf16[4,64,64]{1,2,0:T(8,128)(2,1)S(1)} %fusion.36), channel_id=1, source_target_pairs={{4,0},{6,2},{8,4},{10,6},{12,8},{14,10},{16,12},{18,14},{20,16},{2... | collective-permute-start | bytes 98312 | tf_op jit(solution)/shard_map/ppermute | solution.py:10
  52.8 1.9 %collective-permute-start.14 = (bf16[4,64,64]{1,2,0:T(8,128)(2,1)S(1)}, bf16[4,64,64]{1,2,0:T(8,128)(2,1)S(1)}, u32[]{:S(2)}, u32[]{:S(2)}) collective-permute-start(bf16[4,64,64]{1,2,0:T(8,128)(2,1)S(1)} %fusion.36), channel_id=1, source_target_pairs={{6,0},{8,2},{10,4},{12,6},{14,8},{16,10},{18,12},{20,14},{22,16},{... | collective-permute-start | bytes 98312 | tf_op jit(solution)/shard_map/ppermute | solution.py:10
  55.6 2.4 %collective-permute-start.15 = (bf16[4,64,64]{1,2,0:T(8,128)(2,1)S(1)}, bf16[4,64,64]{1,2,0:T(8,128)(2,1)S(1)}, u32[]{:S(2)}, u32[]{:S(2)}) collective-permute-start(bf16[4,64,64]{1,2,0:T(8,128)(2,1)S(1)} %fusion.36), channel_id=1, source_target_pairs={{8,0},{10,2},{12,4},{14,6},{16,8},{18,10},{20,12},{22,14},{24,16},... | collective-permute-start | bytes 98312 | tf_op jit(solution)/shard_map/ppermute | solution.py:10
  58.9 4.0 %collective-permute-start.4 = (bf16[8,64,64]{1,2,0:T(8,128)(2,1)S(1)}, bf16[8,64,64]{1,2,0:T(8,128)(2,1)S(1)}, u32[]{:S(2)}, u32[]{:S(2)}) collective-permute-start(bf16[8,64,64]{1,2,0:T(8,128)(2,1)S(1)} %bitcast.99), channel_id=1, source_target_pairs={{0,4},{2,6},{4,8},{6,10},{8,12},{10,14},{12,16},{14,18},{16,20},{1... | collective-permute-start | bytes 196616 | tf_op jit(solution)/shard_map/ppermute | solution.py:10
  63.8 3.9 %collective-permute-start.5 = (bf16[8,64,64]{1,2,0:T(8,128)(2,1)S(1)}, bf16[8,64,64]{1,2,0:T(8,128)(2,1)}, u32[]{:S(2)}, u32[]{:S(2)}) collective-permute-start(bf16[8,64,64]{1,2,0:T(8,128)(2,1)S(1)} %bitcast.100), channel_id=1, source_target_pairs={{0,2},{2,4},{4,6},{6,8},{8,10},{10,12},{12,14},{14,16},{16,18},{18... | collective-permute-start | bytes 196616 | tf_op jit(solution)/shard_map/ppermute | solution.py:10
  68.6 6.1 %collective-permute-start.6 = (bf16[8,64,64]{1,2,0:T(8,128)(2,1)S(1)}, bf16[8,64,64]{1,2,0:T(8,128)(2,1)}, u32[]{:S(2)}, u32[]{:S(2)}) collective-permute-start(bf16[8,64,64]{1,2,0:T(8,128)(2,1)S(1)} %bitcast.101), channel_id=1, source_target_pairs={{2,0},{4,2},{6,4},{8,6},{10,8},{12,10},{14,12},{16,14},{18,16},{20... | collective-permute-start | bytes 196616 | tf_op jit(solution)/shard_map/ppermute | solution.py:10
  74.8 2.7 %collective-permute-start.7 = (bf16[8,64,64]{1,2,0:T(8,128)(2,1)S(1)}, bf16[8,64,64]{1,2,0:T(8,128)(2,1)}, u32[]{:S(2)}, u32[]{:S(2)}) collective-permute-start(bf16[8,64,64]{1,2,0:T(8,128)(2,1)S(1)} %bitcast.102), channel_id=1, source_target_pairs={{4,0},{6,2},{8,4},{10,6},{12,8},{14,10},{16,12},{18,14},{20,16},{2... | collective-permute-start | bytes 196616 | tf_op jit(solution)/shard_map/ppermute | solution.py:10
  77.5 3.3 %collective-permute-start.2 = (bf16[16,64,64]{2,1,0:T(8,128)(2,1)S(1)}, bf16[16,64,64]{2,1,0:T(8,128)(2,1)}, u32[]{:S(2)}, u32[]{:S(2)}) collective-permute-start(bf16[16,64,64]{2,1,0:T(8,128)(2,1)S(1)} %convolution_convert_fusion), channel_id=1, source_target_pairs={{0,2},{2,4},{4,6},{6,8},{8,10},{10,12},{12,14},{14,16},{16,18},{18... | collective-permute-start | bytes 393224 | tf_op jit(solution)/shard_map/ppermute | solution.py:21
  80.9 1.8 %gather_fusion.3 = bf16[64,64,64]{1,2,0:T(8,128)(2,1)} fusion(bf16[36,64,64]{1,2,0:T(8,128)(2,1)S(1)} %constant_dynamic-update-slice_fusion.5, s32[1024]{0:T(1024)} %pad_clamp_fusion), kind=kCustom, calls=%fused_computation.3 | custom fusion | bytes 1048832 | tf_op jit(solution)/shard_map/jit(_take)/gather | solution.py:38
  82.7 2.1 %fusion.39 = f32[4,64,64,1]{2,1,3,0:T(8,128)S(1)} fusion(bf16[4,16,64,64]{3,2,1,0:T(8,128)(2,1)} %param.31, bf16[4,16,64,64]{2,3,1,0:T(8,128)(2,1)} %bitcast.103, pred[4,16]{1,0:T(4,128)(4,1)S(1)} %copy-done.18, pred[4,16]{1,0:T(4,128)(4,1)S(1)} %copy-done.19), kind=kOutput, calls=%fused_computation.37 | convolution fusion | flops 34078720 | bytes 1114240 | tf_op jit(solution)/shard_map/tjkm,tjkr->tmr/dot_general | solution.py:42
  84.8 1.4 fusion.58
  86.2 6.7 %collective-permute-start.3 = (bf16[16,64,64]{2,1,0:T(8,128)(2,1)S(1)}, bf16[16,64,64]{2,1,0:T(8,128)(2,1)}, u32[]{:S(2)}, u32[]{:S(2)}) collective-permute-start(bf16[16,64,64]{2,1,0:T(8,128)(2,1)S(1)} %convolution_convert_fusion), channel_id=1, source_target_pairs={{2,0},{4,2},{6,4},{8,6},{10,8},{12,10},{14,12},{16,14},{18,16},{20... | collective-permute-start | bytes 393224 | tf_op jit(solution)/shard_map/ppermute | solution.py:23
  95.8 2.2 %gather_fusion.2 = bf16[128,64,64]{1,2,0:T(8,128)(2,1)} fusion(bf16[40,64,64]{1,2,0:T(8,128)(2,1)S(1)} %constant_dynamic-update-slice_fusion, s32[1024]{0:T(1024)S(1)} %pad_clamp_fusion.1), kind=kCustom, calls=%fused_computation.2 | custom fusion | bytes 2097664 | tf_op jit(solution)/shard_map/jit(_take)/gather | solution.py:38
  98.0 2.5 %fusion.31 = f32[8,64,64,1]{1,2,3,0:T(8,128)S(1)} fusion(f32[8,64,64]{1,2,0:T(8,128)S(1)} %bitcast.106, bf16[8,16,64,64]{3,2,1,0:T(8,128)(2,1)S(1)} %copy-done, bf16[8,16,64,64]{2,3,1,0:T(8,128)(2,1)} %bitcast.95, pred[8,16]{1,0:T(8,128)(4,1)S(1)} %copy-done.16, pred[8,16]{1,0:T(8,128)(4,1)} %iota_compare_fusion.1), kind=kOutput, calls=%fused_computation.29 | convolution fusion | flops 68190208 | bytes 2359552 | tf_op jit(solution)/shard_map/tjkm,tjkr->tmr/dot_general | solution.py:42
  102.6 3.1 %gather_fusion.1 = bf16[256,64,64]{2,1,0:T(8,128)(2,1)} fusion(bf16[48,64,64]{2,1,0:T(8,128)(2,1)S(1)} %pad_maximum_fusion, s32[1024]{0:T(1024)S(1)} %pad_clamp_fusion.2), kind=kCustom, calls=%fused_computation.1 | custom fusion | bytes 4195328 | tf_op jit(solution)/shard_map/jit(_take)/gather | solution.py:38
  105.6 6.4 %copy.31 = bf16[16,16,64,64]{2,3,1,0:T(8,128)(2,1)} copy(bf16[16,16,64,64]{3,2,1,0:T(8,128)(2,1)} %bitcast.93) | data formatting | bytes 4194304 | tf_op jit(solution)/shard_map/jit(_take)/gather | solution.py:38
  112.0 13.4 %fusion.8 = f32[128,256,64]{1,2,0:T(8,128)} fusion(bf16[128,256,256]{2,1,0:T(8,128)(2,1)} %all-gather.2.cloned.1.call-done, bf16[128,256,64]{1,2,0:T(8,128)(2,1)} %gather_fusion, pred[128]{0:T(512)(128)(4,1)S(1)} %get-tuple-element.7), kind=kOutput, calls=%fused_computation.13 | convolution fusion | flops 1075838976 | bytes 29360256 | tf_op jit(solution)/shard_map/bij,bir->bjr/dot_general | solution.py:32
  125.7 17.1 %scatter_fusion = f32[32,256,64]{1,2,0:T(8,128)S(1)} fusion(f32[32,256,64]{1,2,0:T(8,128)S(1)} %broadcast_in_dim.93, s32[128]{0:T(128)S(1)} %copy-done.17, f32[128,256,64]{1,2,0:T(8,128)} %fusion.8), kind=kCustom, calls=%fused_computation.4 | custom fusion | flops 2097152 | bytes 25166336 | tf_op jit(solution)/shard_map/scatter-add | solution.py:34
  142.8 1.3 copy-done.2
  144.2 1.9 %collective-permute-start = (f32[8,256,64]{1,2,0:T(8,128)S(1)}, f32[8,256,64]{1,2,0:T(8,128)S(1)}, u32[]{:S(2)}, u32[]{:S(2)}) collective-permute-start(f32[8,256,64]{1,2,0:T(8,128)S(1)} %slice.22), channel_id=1, source_target_pairs={{0,2},{2,4},{4,6},{6,8},{8,10},{10,12},{12,14},{14,16},{16,18},{18... | collective-permute-start | bytes 1572872 | tf_op jit(solution)/shard_map/ppermute | solution.py:10
  146.1 8.1 %collective-permute-start.1 = (bf16[8,256,64]{1,2,0:T(8,128)(2,1)S(1)}, bf16[8,256,64]{1,2,0:T(8,128)(2,1)S(1)}, u32[]{:S(2)}, u32[]{:S(2)}) collective-permute-start(bf16[8,256,64]{1,2,0:T(8,128)(2,1)S(1)} %slice.32), channel_id=1, source_target_pairs={{2,0},{4,2},{6,4},{8,6},{10,8},{12,10},{14,12},{16,14},{18,16},{20... | collective-permute-start | bytes 786440 | tf_op jit(solution)/shard_map/ppermute | solution.py:10
  154.3 4.6 %fusion.22 = f32[16,64,64]{1,2,0:T(8,128)S(1)} fusion(f32[16,64,64]{1,2,0:T(8,128)S(1)} %bitcast.104, bf16[16,16,64,64]{3,2,1,0:T(8,128)(2,1)} %param.29, bf16[16,16,64,64]{2,3,1,0:T(8,128)(2,1)} %copy.31, pred[16,16]{1,0:T(8,128)(4,1)S(1)} %copy-done.14, pred[16,16]{1,0:T(8,128)(4,1)S(1)} %copy-done.15), kind=kOutput, calls=%fused_computation.24 | convolution fusion | flops 136380416 | bytes 4719104 | tf_op jit(solution)/shard_map/tjkm,tjkr->tmr/dot_general | solution.py:42
  158.9 3.1 %collective-permute-done = f32[8,256,64]{1,2,0:T(8,128)S(1)} collective-permute-done((f32[8,256,64]{1,2,0:T(8,128)S(1)}, f32[8,256,64]{1,2,0:T(8,128)S(1)}, u32[]{:S(2)}, u32[]{:S(2)}) %collective-permute-start) | collective-permute-done | bytes 524320 | tf_op jit(solution)/shard_map/ppermute | solution.py:10
  (103 shorter events, 23.1 us)
Async XLA Ops:
  6.5 91.4 %copy-start = (bf16[8,16,64,64]{3,2,1,0:T(8,128)(2,1)S(1)}, bf16[8,16,64,64]{3,2,1,0:T(8,128)(2,1)}, u32[]{:S(2)}) copy-start(bf16[8,16,64,64]{3,2,1,0:T(8,128)(2,1)} %param.30) | copy-start | bytes 3145732
  6.5 26.9 %copy-start.13 = (s32[4,16]{1,0:T(4,128)S(1)}, s32[4,16]{1,0:T(4,128)}, u32[]{:S(2)}) copy-start(s32[4,16]{1,0:T(4,128)} %param.34) | copy-start | bytes 772
  6.5 27.5 %copy-start.12 = (s32[8,16]{1,0:T(8,128)S(1)}, s32[8,16]{1,0:T(8,128)}, u32[]{:S(2)}) copy-start(s32[8,16]{1,0:T(8,128)} %param.33) | copy-start | bytes 1540
  6.5 28.2 %copy-start.11 = (s32[16,16]{1,0:T(8,128)S(1)}, s32[16,16]{1,0:T(8,128)}, u32[]{:S(2)}) copy-start(s32[16,16]{1,0:T(8,128)} %param.32) | copy-start | bytes 3076
  6.6 105.5 %all-gather.2.cloned.1.call-start = ((), (), s32[]{:S(2)}) async-start(), calls=%async_computation | async-start | bytes 25165824 | tf_op jit(solution)/shard_map/all_gather | solution.py:112
  11.2 36.8 %collective-permute-start.8 = (bf16[4,64,64]{1,2,0:T(8,128)(2,1)S(1)}, bf16[4,64,64]{1,2,0:T(8,128)(2,1)S(1)}, u32[]{:S(2)}, u32[]{:S(2)}) collective-permute-start(bf16[4,64,64]{1,2,0:T(8,128)(2,1)S(1)} %fusion.36), channel_id=1, source_target_pairs={{0,8},{2,10},{4,12},{6,14},{8,16},{10,18},{12,20},{14,22},{16,24},... | collective-permute-start | bytes 98312 | tf_op jit(solution)/shard_map/ppermute | solution.py:10
  14.6 38.3 %collective-permute-start.9 = (bf16[4,64,64]{1,2,0:T(8,128)(2,1)S(1)}, bf16[4,64,64]{1,2,0:T(8,128)(2,1)}, u32[]{:S(2)}, u32[]{:S(2)}) collective-permute-start(bf16[4,64,64]{1,2,0:T(8,128)(2,1)S(1)} %fusion.36), channel_id=1, source_target_pairs={{0,6},{2,8},{4,10},{6,12},{8,14},{10,16},{12,18},{14,20},{16,22},{... | collective-permute-start | bytes 98312 | tf_op jit(solution)/shard_map/ppermute | solution.py:10
  20.5 35.1 %collective-permute-start.10 = (bf16[4,64,64]{1,2,0:T(8,128)(2,1)S(1)}, bf16[4,64,64]{1,2,0:T(8,128)(2,1)}, u32[]{:S(2)}, u32[]{:S(2)}) collective-permute-start(bf16[4,64,64]{1,2,0:T(8,128)(2,1)S(1)} %fusion.36), channel_id=1, source_target_pairs={{0,4},{2,6},{4,8},{6,10},{8,12},{10,14},{12,16},{14,18},{16,20},{1... | collective-permute-start | bytes 98312 | tf_op jit(solution)/shard_map/ppermute | solution.py:10
  23.3 35.6 %collective-permute-start.11 = (bf16[4,64,64]{1,2,0:T(8,128)(2,1)S(1)}, bf16[4,64,64]{1,2,0:T(8,128)(2,1)}, u32[]{:S(2)}, u32[]{:S(2)}) collective-permute-start(bf16[4,64,64]{1,2,0:T(8,128)(2,1)S(1)} %fusion.36), channel_id=1, source_target_pairs={{0,2},{2,4},{4,6},{6,8},{8,10},{10,12},{12,14},{14,16},{16,18},{18... | collective-permute-start | bytes 98312 | tf_op jit(solution)/shard_map/ppermute | solution.py:10
  26.5 37.3 %collective-permute-start.12 = (bf16[4,64,64]{1,2,0:T(8,128)(2,1)S(1)}, bf16[4,64,64]{1,2,0:T(8,128)(2,1)}, u32[]{:S(2)}, u32[]{:S(2)}) collective-permute-start(bf16[4,64,64]{1,2,0:T(8,128)(2,1)S(1)} %fusion.36), channel_id=1, source_target_pairs={{2,0},{4,2},{6,4},{8,6},{10,8},{12,10},{14,12},{16,14},{18,16},{20... | collective-permute-start | bytes 98312 | tf_op jit(solution)/shard_map/ppermute | solution.py:10
  45.1 13.8 %copy-start.6 = (bf16[8,64,64]{2,1,0:T(8,128)(2,1)S(1)}, bf16[8,64,64]{2,1,0:T(8,128)(2,1)}, u32[]{:S(2)}) copy-start(bf16[8,64,64]{2,1,0:T(8,128)(2,1)} %copy-done.5) | copy-start | bytes 196612
  45.1 37.5 %copy-start.18 = (pred[4,16]{1,0:T(4,128)(4,1)S(1)}, pred[4,16]{1,0:T(4,128)(4,1)}, u32[]{:S(2)}) copy-start(pred[4,16]{1,0:T(4,128)(4,1)} %get-tuple-element.13) | copy-start | bytes 196
  45.1 37.5 %copy-start.19 = (pred[4,16]{1,0:T(4,128)(4,1)S(1)}, pred[4,16]{1,0:T(4,128)(4,1)}, u32[]{:S(2)}) copy-start(pred[4,16]{1,0:T(4,128)(4,1)} %iota_compare_fusion.2) | copy-start | bytes 196
  48.6 20.0 %collective-permute-start.13 = (bf16[4,64,64]{1,2,0:T(8,128)(2,1)S(1)}, bf16[4,64,64]{1,2,0:T(8,128)(2,1)S(1)}, u32[]{:S(2)}, u32[]{:S(2)}) collective-permute-start(bf16[4,64,64]{1,2,0:T(8,128)(2,1)S(1)} %fusion.36), channel_id=1, source_target_pairs={{4,0},{6,2},{8,4},{10,6},{12,8},{14,10},{16,12},{18,14},{20,16},{2... | collective-permute-start | bytes 98312 | tf_op jit(solution)/shard_map/ppermute | solution.py:10
  52.8 22.0 %collective-permute-start.14 = (bf16[4,64,64]{1,2,0:T(8,128)(2,1)S(1)}, bf16[4,64,64]{1,2,0:T(8,128)(2,1)S(1)}, u32[]{:S(2)}, u32[]{:S(2)}) collective-permute-start(bf16[4,64,64]{1,2,0:T(8,128)(2,1)S(1)} %fusion.36), channel_id=1, source_target_pairs={{6,0},{8,2},{10,4},{12,6},{14,8},{16,10},{18,12},{20,14},{22,16},{... | collective-permute-start | bytes 98312 | tf_op jit(solution)/shard_map/ppermute | solution.py:10
  55.6 21.9 %collective-permute-start.15 = (bf16[4,64,64]{1,2,0:T(8,128)(2,1)S(1)}, bf16[4,64,64]{1,2,0:T(8,128)(2,1)S(1)}, u32[]{:S(2)}, u32[]{:S(2)}) collective-permute-start(bf16[4,64,64]{1,2,0:T(8,128)(2,1)S(1)} %fusion.36), channel_id=1, source_target_pairs={{8,0},{10,2},{12,4},{14,6},{16,8},{18,10},{20,12},{22,14},{24,16},... | collective-permute-start | bytes 98312 | tf_op jit(solution)/shard_map/ppermute | solution.py:10
  58.9 27.2 %collective-permute-start.4 = (bf16[8,64,64]{1,2,0:T(8,128)(2,1)S(1)}, bf16[8,64,64]{1,2,0:T(8,128)(2,1)S(1)}, u32[]{:S(2)}, u32[]{:S(2)}) collective-permute-start(bf16[8,64,64]{1,2,0:T(8,128)(2,1)S(1)} %bitcast.99), channel_id=1, source_target_pairs={{0,4},{2,6},{4,8},{6,10},{8,12},{10,14},{12,16},{14,18},{16,20},{1... | collective-permute-start | bytes 196616 | tf_op jit(solution)/shard_map/ppermute | solution.py:10
  63.8 29.1 %collective-permute-start.5 = (bf16[8,64,64]{1,2,0:T(8,128)(2,1)S(1)}, bf16[8,64,64]{1,2,0:T(8,128)(2,1)}, u32[]{:S(2)}, u32[]{:S(2)}) collective-permute-start(bf16[8,64,64]{1,2,0:T(8,128)(2,1)S(1)} %bitcast.100), channel_id=1, source_target_pairs={{0,2},{2,4},{4,6},{6,8},{8,10},{10,12},{12,14},{14,16},{16,18},{18... | collective-permute-start | bytes 196616 | tf_op jit(solution)/shard_map/ppermute | solution.py:10
  68.6 25.3 %collective-permute-start.6 = (bf16[8,64,64]{1,2,0:T(8,128)(2,1)S(1)}, bf16[8,64,64]{1,2,0:T(8,128)(2,1)}, u32[]{:S(2)}, u32[]{:S(2)}) collective-permute-start(bf16[8,64,64]{1,2,0:T(8,128)(2,1)S(1)} %bitcast.101), channel_id=1, source_target_pairs={{2,0},{4,2},{6,4},{8,6},{10,8},{12,10},{14,12},{16,14},{18,16},{20... | collective-permute-start | bytes 196616 | tf_op jit(solution)/shard_map/ppermute | solution.py:10
  74.8 20.1 %collective-permute-start.7 = (bf16[8,64,64]{1,2,0:T(8,128)(2,1)S(1)}, bf16[8,64,64]{1,2,0:T(8,128)(2,1)}, u32[]{:S(2)}, u32[]{:S(2)}) collective-permute-start(bf16[8,64,64]{1,2,0:T(8,128)(2,1)S(1)} %bitcast.102), channel_id=1, source_target_pairs={{4,0},{6,2},{8,4},{10,6},{12,8},{14,10},{16,12},{18,14},{20,16},{2... | collective-permute-start | bytes 196616 | tf_op jit(solution)/shard_map/ppermute | solution.py:10
  77.5 23.8 %collective-permute-start.2 = (bf16[16,64,64]{2,1,0:T(8,128)(2,1)S(1)}, bf16[16,64,64]{2,1,0:T(8,128)(2,1)}, u32[]{:S(2)}, u32[]{:S(2)}) collective-permute-start(bf16[16,64,64]{2,1,0:T(8,128)(2,1)S(1)} %convolution_convert_fusion), channel_id=1, source_target_pairs={{0,2},{2,4},{4,6},{6,8},{8,10},{10,12},{12,14},{14,16},{16,18},{18... | collective-permute-start | bytes 393224 | tf_op jit(solution)/shard_map/ppermute | solution.py:21
  82.7 15.3 %copy-start.16 = (pred[8,16]{1,0:T(8,128)(4,1)S(1)}, pred[8,16]{1,0:T(8,128)(4,1)}, u32[]{:S(2)}) copy-start(pred[8,16]{1,0:T(8,128)(4,1)} %get-tuple-element.11) | copy-start | bytes 388
  86.2 15.2 %collective-permute-start.3 = (bf16[16,64,64]{2,1,0:T(8,128)(2,1)S(1)}, bf16[16,64,64]{2,1,0:T(8,128)(2,1)}, u32[]{:S(2)}, u32[]{:S(2)}) collective-permute-start(bf16[16,64,64]{2,1,0:T(8,128)(2,1)S(1)} %convolution_convert_fusion), channel_id=1, source_target_pairs={{2,0},{4,2},{6,4},{8,6},{10,8},{12,10},{14,12},{16,14},{18,16},{20... | collective-permute-start | bytes 393224 | tf_op jit(solution)/shard_map/ppermute | solution.py:23
  98.0 2.5 %copy-start.9 = (bf16[16,64,64]{2,1,0:T(8,128)(2,1)S(1)}, bf16[16,64,64]{2,1,0:T(8,128)(2,1)}, u32[]{:S(2)}) copy-start(bf16[16,64,64]{2,1,0:T(8,128)(2,1)} %param.28) | copy-start | bytes 393220
  112.0 13.6 %copy-start.17 = (s32[128]{0:T(128)S(1)}, s32[128]{0:T(128)}, u32[]{:S(2)}) copy-start(s32[128]{0:T(128)} %broadcast_subtract_fusion.3) | copy-start | bytes 1540
  125.7 28.6 %copy-start.14 = (pred[16,16]{1,0:T(8,128)(4,1)S(1)}, pred[16,16]{1,0:T(8,128)(4,1)}, u32[]{:S(2)}) copy-start(pred[16,16]{1,0:T(8,128)(4,1)} %get-tuple-element.9) | copy-start | bytes 772
  125.7 28.6 %copy-start.15 = (pred[16,16]{1,0:T(8,128)(4,1)S(1)}, pred[16,16]{1,0:T(8,128)(4,1)}, u32[]{:S(2)}) copy-start(pred[16,16]{1,0:T(8,128)(4,1)} %get-tuple-element.15) | copy-start | bytes 772
  144.2 17.9 %collective-permute-start = (f32[8,256,64]{1,2,0:T(8,128)S(1)}, f32[8,256,64]{1,2,0:T(8,128)S(1)}, u32[]{:S(2)}, u32[]{:S(2)}) collective-permute-start(f32[8,256,64]{1,2,0:T(8,128)S(1)} %slice.22), channel_id=1, source_target_pairs={{0,2},{2,4},{4,6},{6,8},{8,10},{10,12},{12,14},{14,16},{16,18},{18... | collective-permute-start | bytes 1572872 | tf_op jit(solution)/shard_map/ppermute | solution.py:10
  146.1 12.8 %collective-permute-start.1 = (bf16[8,256,64]{1,2,0:T(8,128)(2,1)S(1)}, bf16[8,256,64]{1,2,0:T(8,128)(2,1)S(1)}, u32[]{:S(2)}, u32[]{:S(2)}) collective-permute-start(bf16[8,256,64]{1,2,0:T(8,128)(2,1)S(1)} %slice.32), channel_id=1, source_target_pairs={{2,0},{4,2},{6,4},{8,6},{10,8},{12,10},{14,12},{16,14},{18,16},{20... | collective-permute-start | bytes 786440 | tf_op jit(solution)/shard_map/ppermute | solution.py:10
  154.3 7.8 %copy-start.3 = (f32[32,256,64]{1,2,0:T(8,128)S(1)}, f32[32,256,64]{1,2,0:T(8,128)}, u32[]{:S(2)}) copy-start(f32[32,256,64]{1,2,0:T(8,128)} %copy-done.2) | copy-start | bytes 6291460
  154.3 7.8 %copy-start.7 = (bf16[16,256,64]{1,2,0:T(8,128)(2,1)S(1)}, bf16[16,256,64]{1,2,0:T(8,128)(2,1)}, u32[]{:S(2)}) copy-start(bf16[16,256,64]{1,2,0:T(8,128)(2,1)} %param.24) | copy-start | bytes 1572868
  154.3 9.3 %copy-start.1 = (bf16[8,16,64,64]{3,2,1,0:T(8,128)(2,1)S(1)}, bf16[8,16,64,64]{3,2,1,0:T(8,128)(2,1)}, u32[]{:S(2)}) copy-start(bf16[8,16,64,64]{3,2,1,0:T(8,128)(2,1)} %param.30) | copy-start | bytes 3145732
  (5 other events, 5.2 us)
Sparse Core Ops, SparseCore 0:
  9.0 35.0 all-gather.1
where the time goes:
time: 172 us; the launch traced here: 170 us
  starting transfers between devices  66.9 us (39%)
  local copies, waits for them, and re-layouts  30.9 us (18%)
  matrix products  28.1 us (16%)
  other arithmetic  24.4 us (14%)
  between operations  14.5 us (8%)
  waiting for transfers between devices  3.81 us (2%)
  blocking collectives  1.82 us (1%)
    ppermute x14, starting transfers between devices, passed_along(): return lax.ppermute(block, axis, route)  56.8 us
    scatter-add x1, other arithmetic, near_terms(): jax.ops.segment_sum(products, slots, num_segments=leaf_clusters + 2 * mar...  17.1 us
    gather x4, local copies, waits for them, and re-layouts, couple_level(): picked = jnp.take(coeffs, (sources - lowest).reshape(-1), axis=0)  13.4 us
    dot_general x1, matrix products, near_terms(): jnp.einsum('bij,bir->bjr', blocks, picked, preferred_element_type=jnp.flo...  13.4 us
    unnamed x57, local copies, waits for them, and re-layouts  12.3 us
    dot_general x3, matrix products, couple_level(): jnp.einsum('tjkm,tjkr->tmr', blocks, picked, preferred_element_type=jnp.f...  9.14 us
    ppermute x1, starting transfers between devices, extended(): lax.ppermute(head, axis, [((i + 1) % count, i) for i in range(ends)])  6.75 us
  transfers between devices with their start and end apart: 17, of which 1 were waited for; matrix products, arithmetic and copies ran while one was open for 28% of the time, Pallas kernels for 0%

commit v1 on v0

v1 whole, which is shorter than its diff:
```python
import jax
import jax.numpy as jnp
from jax import lax
from jax.experimental import pallas as pl
from jax.experimental.pallas import tpu as pltpu
from jax.sharding import PartitionSpec as P

F32 = jnp.float32
BF16 = jnp.bfloat16
VM = pl.BlockSpec(memory_space=pltpu.VMEM)
SM = pl.BlockSpec(memory_space=pltpu.SMEM)
HB = pl.BlockSpec(memory_space=pl.ANY)

N_PACK = 14
N_FAR_PACK = 10
CHUNKS = 8
MIDDLE_AT = 48
TOP_AT = MIDDLE_AT + 40
ZERO_AT = TOP_AT + 36


def ring(block, distance):
    count = lax.axis_size("leaf")
    return lax.ppermute(block, "leaf", [(i, (i + distance) % count) for i in range(count)])


def swapped(block):
    return lax.ppermute(block, "rhs", [(0, 1), (1, 0)])


def mm(a, b):
    return lax.dot_general(a, b, (((1,), (0,)), ((), ())), preferred_element_type=F32)


def mm_t(a, b):
    return lax.dot_general(a, b, (((1,), (1,)), ((), ())), preferred_element_type=F32)


def coeff_kernel(x, basis, lift_leaf, lift_middle, pack):
    for q in range(4):
        middles = []
        for p in (2 * q, 2 * q + 1):
            pair = [
                mm_t(x[:, l * 256 : (l + 1) * 256], basis[l]) for l in (2 * p, 2 * p + 1)
            ]
            block = jnp.concatenate(pair, axis=1).astype(BF16)
            pack[p] = block
            middles.append(mm(block, lift_leaf[p]))
        pack[8 + q] = jnp.concatenate(middles, axis=1).astype(BF16)
    for h in range(2):
        tops = [mm(pack[8 + q], lift_middle[q]) for q in (2 * h, 2 * h + 1)]
        pack[12 + h] = jnp.concatenate(tops, axis=1).astype(BF16)


def near_kernel(row, col, x, xp, blocks, own, halo, other, held, acc, sems):
    per = blocks.shape[0] // CHUNKS
    copies = [
        pltpu.make_async_copy(
            blocks.at[pl.ds(c * per, per)], held.at[pl.ds(c * per, per)], sems.at[c]
        )
        for c in range(CHUNKS)
    ]
    for c in copies:
        c.start()
    acc[...] = jnp.zeros_like(acc)
    device = row[0] // 16
    for c in range(CHUNKS):
        copies[c].wait()
        for b in range(c * per, (c + 1) * per):
            at = pl.multiple_of((row[b] - device * 16) * 256, 256)
            slot = col[b] - device * 16 + 8
            left = jnp.concatenate([x[:, pl.ds(at, 256)], xp[:, pl.ds(at, 256)]], axis=0)
            acc[slot] += mm(left, held[b])
    own[...] = acc[8:24, :64]
    halo[:8] = acc[:8, :64]
    halo[8:] = acc[24:, :64]
    other[...] = acc[:, 64:].astype(BF16)


def pack_kernel(left, own, right, up, down):
    up[0:2] = left[12:14]
    up[2:4] = own[12:14]
    up[4:10] = right[8:14]
    down[0:6] = left[8:14]
    down[6:8] = own[12:14]
    down[8:10] = right[12:14]


def halo_kernel(halo, received, low, high):
    low[...] = (halo[:8] + received[:8].astype(F32)).astype(BF16)
    high[...] = (halo[8:] + received[24:].astype(F32)).astype(BF16)


def far_kernel(
    row,
    list_leaf,
    list_middle,
    list_top,
    count_leaf,
    count_middle,
    count_top,
    pack,
    left,
    right,
    far_left,
    far_right,
    spread_middle,
    spread_leaf,
    bases,
    near,
    received,
    couple_leaf,
    couple_middle,
    couple_top,
    out,
    held_leaf,
    held_middle,
    held_top,
    dup,
    sems,
):
    copies_top = pltpu.make_async_copy(couple_top, held_top, sems.at[0])
    copies_middle = pltpu.make_async_copy(couple_middle, held_middle, sems.at[1])
    copies_leaf = [
        pltpu.make_async_copy(
            couple_leaf.at[pl.ds(4 * c, 4)], held_leaf.at[pl.ds(4 * c, 4)], sems.at[2 + c]
        )
        for c in range(4)
    ]
    copies_top.start()
    copies_middle.start()
    for c in copies_leaf:
        c.start()
    device = row[0] // 16
    first = lax.broadcasted_iota(jnp.int32, (64, 128), 1) < 64

    def double(at, block):
        turned = jnp.concatenate([block[:, 64:], block[:, :64]], axis=1)
        dup[at] = jnp.where(first, block, turned)
        dup[at + 1] = jnp.where(first, turned, block)

    for i in range(2):
        for k, (ref, at) in enumerate(
            (
                (far_left, 0),
                (far_left, 2),
                (far_left, 8),
                (left, 12),
                (pack, 12),
                (right, 12),
                (far_right, 4),
                (far_right, 6),
                (far_right, 8),
            )
        ):
            double(TOP_AT + 4 * k + 2 * i, ref[at + i])
    for i in range(4):
        for k, (ref, at) in enumerate(
            ((far_left, 4), (left, 8), (pack, 8), (right, 8), (far_right, 0))
        ):
            double(MIDDLE_AT + 8 * k + 2 * i, ref[at + i])
    for i in range(8):
        for k, ref in enumerate((left, pack, right)):
            double(16 * k + 2 * i, ref[i])
    dup[ZERO_AT] = jnp.zeros((64, 128), BF16)

    def coupled(held, lists, counts, t, base):
        live = counts[t]

        def source(j):
            return jnp.where(j < live, lists[t, j] + base, ZERO_AT)

        gathered = jnp.concatenate(
            [
                jnp.where(first, dup[source(j)], dup[source(j + 1)])
                for j in range(0, 16, 2)
            ],
            axis=1,
        )
        return mm(gathered, held[t])

    copies_top.wait()
    down_top = [
        coupled(held_top, list_top, count_top, t, TOP_AT + 16 - 4 * device).astype(BF16)
        for t in range(4)
    ]
    copies_middle.wait()
    down_middle = [
        (
            coupled(
                held_middle, list_middle, count_middle, t, MIDDLE_AT + 16 - 8 * device
            )
            + mm_t(down_top[t // 2], spread_middle[t])
        ).astype(BF16)
        for t in range(8)
    ]
    for t in range(16):
        if t % 4 == 0:
            copies_leaf[t // 4].wait()
        down = (
            coupled(held_leaf, list_leaf, count_leaf, t, 16 - 16 * device)
            + mm_t(down_middle[t // 2], spread_leaf[t])
        ).astype(BF16)
        out[t] = mm(down, bases[t]) + (near[t] + received[8 + t].astype(F32))


def final_kernel(total, from_left, from_right, out):
    for l in range(16):
        halo = from_left[l] if l < 8 else from_right[l - 8]
        out[:, l * 256 : (l + 1) * 256] = (total[l] + halo.astype(F32)).astype(BF16)


def shaped(*shape, dtype=BF16):
    return jax.ShapeDtypeStruct(shape, dtype)


def call(name, kernel, specs, outs, *args, scratch=(), mib=16, flops=0, moved=0):
    return pl.pallas_call(
        kernel,
        name=name,
        in_specs=specs,
        out_shape=outs,
        out_specs=jax.tree.map(lambda _: VM, outs),
        scratch_shapes=scratch,
        compiler_params=pltpu.CompilerParams(vmem_limit_bytes=mib << 20),
        cost_estimate=pl.CostEstimate(flops=flops, bytes_accessed=moved, transcendentals=0),
    )(*args)


def shards(
    operand,
    near_blocks,
    near_row,
    near_column,
    row_basis,
    leaf_column_bases,
    lift_leaf,
    lift_middle,
    spread_middle,
    spread_leaf,
    couple_leaf,
    couple_middle,
    couple_top,
    list_leaf,
    list_middle,
    list_top,
    count_leaf,
    count_middle,
    count_top,
):
    x = operand.T
    xp = swapped(x)
    pack = call(
        "coeff",
        coeff_kernel,
        [VM] * 4,
        shaped(N_PACK, 64, 128),
        x,
        jnp.swapaxes(row_basis, 1, 2),
        lift_leaf.reshape(8, 128, 64),
        lift_middle.reshape(4, 128, 64),
        flops=40_000_000,
        moved=2 << 20,
    )
    left, right = ring(pack, 1), ring(pack, -1)
    own, halo, other = call(
        "near",
        near_kernel,
        [SM, SM, VM, VM, HB],
        [shaped(16, 64, 256, dtype=F32), shaped(16, 64, 256, dtype=F32), shaped(32, 64, 256)],
        near_row,
        near_column,
        x,
        xp,
        near_blocks,
        scratch=[
            pltpu.VMEM((64, 256, 256), BF16),
            pltpu.VMEM((32, 128, 256), F32),
            pltpu.SemaphoreType.DMA((CHUNKS,)),
        ],
        mib=24,
        flops=1_100_000_000,
        moved=14 << 20,
    )
    received = swapped(other)
    up, down = call(
        "pack",
        pack_kernel,
        [VM] * 3,
        [shaped(N_FAR_PACK, 64, 128)] * 2,
        left,
        pack,
        right,
        moved=1 << 20,
    )
    far_left, far_right = ring(up, 3), ring(down, -3)
    low, high = call(
        "halo",
        halo_kernel,
        [VM] * 2,
        [shaped(8, 64, 256)] * 2,
        halo,
        received,
        moved=2 << 20,
    )
    from_left, from_right = ring(high, 1), ring(low, -1)
    total = call(
        "far",
        far_kernel,
        [SM] * 7 + [VM] * 10 + [HB] * 3,
        shaped(16, 64, 256, dtype=F32),
        near_row,
        list_leaf,
        list_middle,
        list_top,
        count_leaf,
        count_middle,
        count_top,
        pack,
        left,
        right,
        far_left,
        far_right,
        spread_middle,
        spread_leaf,
        jnp.swapaxes(leaf_column_bases, 1, 2),
        own,
        received,
        couple_leaf.reshape(16, 1024, 64),
        couple_middle.reshape(8, 1024, 64),
        couple_top.reshape(4, 1024, 64),
        scratch=[
            pltpu.VMEM((16, 1024, 64), BF16),
            pltpu.VMEM((8, 1024, 64), BF16),
            pltpu.VMEM((4, 1024, 64), BF16),
            pltpu.VMEM((ZERO_AT + 1, 64, 128), BF16),
            pltpu.SemaphoreType.DMA((6,)),
        ],
        mib=24,
        flops=300_000_000,
        moved=14 << 20,
    )
    out = call(
        "final",
        final_kernel,
        [VM] * 3,
        shaped(64, 4096),
        total,
        from_left,
        from_right,
        moved=2 << 20,
    )
    return out.T


def solution(mesh):
    return jax.shard_map(
        shards,
        mesh=mesh,
        in_specs=(
            P("leaf", "rhs"),
            P(("leaf", "rhs"), None, None),
            P(("leaf", "rhs")),
            P(("leaf", "rhs")),
            P("leaf", None, None),
            P("leaf", None, None),
            P("leaf", None, None),
            P("leaf", None, None),
            P("leaf", None, None),
            P("leaf", None, None),
            P("leaf", None, None, None),
            P("leaf", None, None, None),
            P("leaf", None, None, None),
            P("leaf", None),
            P("leaf", None),
            P("leaf", None),
            P("leaf"),
            P("leaf"),
            P("leaf"),
        ),
        out_specs=P("leaf", "rhs"),
        check_vma=False,
    )
```

time: 172 us -> 54.1 us (0.31)
  the two profiles are of different devices: /device:TPU:16 before, /device:TPU:0 now
where the time goes in v1:
time: 54.1 us; the launch traced here: 53.9 us
  starting transfers between devices  23 us (43%)
  Pallas kernels  13.3 us (25%)
  waiting for transfers between devices  11.6 us (21%)
  local copies, waits for them, and re-layouts  5.82 us (11%)
    ppermute x6, starting transfers between devices, ring(): lax.ppermute(block, 'leaf', [(i, (i + distance) % count) for i in range(c...  22.8 us
    pallas_call x6, Pallas kernels, call(): pl.pallas_call(kernel, name=name, in_specs=specs, out_shape=outs, out_spe...  13.3 us
    ppermute x6, waiting for transfers between devices, ring(): lax.ppermute(block, 'leaf', [(i, (i + distance) % count) for i in range(c...  9.48 us
    unnamed x40, local copies, waits for them, and re-layouts  5.82 us
    ppermute x2, waiting for transfers between devices, swapped(): return lax.ppermute(block, 'rhs', [(0, 1), (1, 0)])  2.12 us
  transfers between devices with their start and end apart: 8, of which 3 were waited for; matrix products, arithmetic and copies ran while one was open for 0% of the time, Pallas kernels for 15%

profile of v1, /device:TPU:0, one launch (start us, length us, event | category | flops | bytes accessed | tf_op | source)
XLA Modules:
  0.0 53.9 jit_solution(423847646228782334)
XLA Ops:
  0.0 0.0 collective-permute-start.4
  0.0 2.1 %collective-permute-done.4.xp = bf16[64,4096]{1,0:T(8,128)(2,1)S(1)} collective-permute-done((bf16[64,4096]{1,0:T(8,128)(2,1)}, bf16[64,4096]{1,0:T(8,128)(2,1)S(1)}, u32[]{:S(2)}, u32[]{:S(2)}) %collective-permute-start.4) | collective-permute-done | bytes 524320 | tf_op jit(solution)/shard_map/ppermute | solution.py:28
  2.1 3.4 %copy-done = bf16[64,256,256]{2,1,0:T(8,128)(2,1)S(1)} copy-done((bf16[64,256,256]{2,1,0:T(8,128)(2,1)S(1)}, bf16[64,256,256]{2,1,0:T(8,128)(2,1)}, u32[]{:S(2)}) %copy-start) | copy-done | bytes 8388632
  5.5 1.0 %copy-done.2 = bf16[4096,64]{0,1:T(8,128)(2,1)S(1)} copy-done((bf16[4096,64]{0,1:T(8,128)(2,1)S(1)}, bf16[4096,64]{0,1:T(8,128)(2,1)}, u32[]{:S(2)}) %copy-start.2) | copy-done | bytes 524312
  6.5 0.7 %copy-done.14 = s32[64]{0:T(128)S(1)} copy-done((s32[64]{0:T(128)S(1)}, s32[64]{0:T(128)}, u32[]{:S(2)}) %copy-start.14) | copy-done | bytes 280
  7.2 0.7 %copy-done.16 = s32[64]{0:T(128)S(1)} copy-done((s32[64]{0:T(128)S(1)}, s32[64]{0:T(128)}, u32[]{:S(2)}) %copy-start.16) | copy-done | bytes 280
  7.9 4.3 %near.1 = (f32[16,64,256]{2,1,0:T(8,128)S(1)}, f32[16,64,256]{2,1,0:T(8,128)S(1)}, bf16[32,64,256]{2,1,0:T(8,128)(2,1)S(1)}) custom-call(s32[64]{0:T(128)S(1)} %copy-done.14, s32[64]{0:T(128)S(1)} %copy-done.16, bf16[64,4096]{1,0:T(8,128)(2,1)S(1)} %bitcast.11, bf16[64,4096]{1,0:T(8,128)(2,1)S(1)} %collective-permute-done.4.xp, bf16[64,256,256]{2,1,0:T(8,128)(2,1)S(1)} %copy-done), custom_call_target="tpu_custom_call" | custom-call | flops 1100000000 | bytes 14680064 | tf_op jit(solution)/shard_map/near/pallas_call | solution.py:218
  12.2 0.0 copy-start.1
  12.3 0.0 copy-start.8
  12.3 0.0 copy-start.11
  12.3 0.0 copy-start.12
  12.3 0.0 copy-start.13
  12.3 0.0 copy-start.15
  12.3 0.0 copy-start.17
  12.3 0.0 copy-start.18
  12.3 0.0 copy-start.19
  12.3 0.2 collective-permute-start.5
  12.6 2.0 %coeff.1.own.pack = bf16[14,64,128]{2,1,0:T(8,128)(2,1)S(1)} custom-call(bf16[64,4096]{1,0:T(8,128)(2,1)S(1)} %bitcast.12, bf16[16,64,256]{2,1,0:T(8,128)(2,1)S(1)} %bitcast.15, bf16[8,128,64]{2,1,0:T(8,128)(2,1)S(1)} %bitcast.17, bf16[4,128,64]{2,1,0:T(8,128)(2,1)S(1)} %bitcast.18), custom_call_target="tpu_custom_call" | custom-call | flops 40000000 | bytes 2097152 | tf_op jit(solution)/shard_map/coeff/pallas_call | solution.py:218
  14.6 8.9 %collective-permute-start.1 = (bf16[14,64,128]{2,1,0:T(8,128)(2,1)S(1)}, bf16[14,64,128]{2,1,0:T(8,128)(2,1)S(1)}, u32[]{:S(2)}, u32[]{:S(2)}) collective-permute-start(bf16[14,64,128]{2,1,0:T(8,128)(2,1)S(1)} %coeff.1.own.pack), channel_id=1, source_target_pairs={{0,126},{2,0},{4,2},{6,4},{8,6},{10,8},{12,10},{14,12},{16,14},{18... | collective-permute-start | bytes 688136 | tf_op jit(solution)/shard_map/ppermute | solution.py:24
  23.5 0.0 collective-permute-start
  23.5 0.0 collective-permute-done.5.received
  23.5 0.1 halo.1
  23.6 0.1 collective-permute-start.6
  23.7 7.5 %collective-permute-start.7 = (bf16[8,64,256]{2,1,0:T(8,128)(2,1)S(1)}, bf16[8,64,256]{2,1,0:T(8,128)(2,1)S(1)}, u32[]{:S(2)}, u32[]{:S(2)}) collective-permute-start(bf16[8,64,256]{2,1,0:T(8,128)(2,1)S(1)} %get-tuple-element.18), channel_id=1, source_target_pairs={{0,126},{2,0},{4,2},{6,4},{8,6},{10,8},{12,10},{14,12},{16,14},{18... | collective-permute-start | bytes 786440 | tf_op jit(solution)/shard_map/ppermute | solution.py:24
  31.2 0.0 collective-permute-done.1.right
  31.2 6.2 %collective-permute-done.left = bf16[14,64,128]{2,1,0:T(8,128)(2,1)S(1)} collective-permute-done((bf16[14,64,128]{2,1,0:T(8,128)(2,1)S(1)}, bf16[14,64,128]{2,1,0:T(8,128)(2,1)S(1)}, u32[]{:S(2)}, u32[]{:S(2)}) %collective-permute-start) | collective-permute-done | bytes 229408 | tf_op jit(solution)/shard_map/ppermute | solution.py:24
  37.4 0.1 collective-permute-start.2
  37.5 6.2 %collective-permute-start.3 = (bf16[10,64,128]{2,1,0:T(8,128)(2,1)S(1)}, bf16[10,64,128]{2,1,0:T(8,128)(2,1)S(1)}, u32[]{:S(2)}, u32[]{:S(2)}) collective-permute-start(bf16[10,64,128]{2,1,0:T(8,128)(2,1)S(1)} %get-tuple-element.13), channel_id=1, source_target_pairs={{0,122},{2,124},{4,126},{6,0},{8,2},{10,4},{12,6},{14,8},{16,10},{... | collective-permute-start | bytes 491528 | tf_op jit(solution)/shard_map/ppermute | solution.py:24
  43.7 3.3 %collective-permute-done.2.far_left = bf16[10,64,128]{2,1,0:T(8,128)(2,1)S(1)} collective-permute-done((bf16[10,64,128]{2,1,0:T(8,128)(2,1)S(1)}, bf16[10,64,128]{2,1,0:T(8,128)(2,1)S(1)}, u32[]{:S(2)}, u32[]{:S(2)}) %collective-permute-start.2) | collective-permute-done | bytes 163872 | tf_op jit(solution)/shard_map/ppermute | solution.py:24
  47.1 5.8 %far.1.total = f32[16,64,256]{2,1,0:T(8,128)S(1)} custom-call(s32[64]{0:T(128)S(1)} %copy-done.15, s32[16,16]{1,0:T(8,128)S(1)} %copy-done.11, s32[8,16]{1,0:T(8,128)S(1)} %copy-done.12, s32[4,16]{1,0:T(4,128)S(1)} %copy-done.13, s32[16]{0:T(128)S(1)} %copy-done.17, s32[8]{0:T(128)S(1)} %copy-done.18, s32[4]{0:T(128)S(1)} %copy-done.19, ...), custom_call_target="tpu_custom_call" | custom-call | flops 300000000 | bytes 14680064 | tf_op jit(solution)/shard_map/far/pallas_call | solution.py:218
  53.0 0.0 collective-permute-done.6.from_left
  53.0 0.9 %final.1 = bf16[64,4096]{1,0:T(8,128)(2,1)} custom-call(f32[16,64,256]{2,1,0:T(8,128)S(1)} %far.1.total, bf16[8,64,256]{2,1,0:T(8,128)(2,1)S(1)} %collective-permute-done.6.from_left, bf16[8,64,256]{2,1,0:T(8,128)(2,1)S(1)} %collective-permute-done.7.from_right), custom_call_target="tpu_custom_call" | custom-call | bytes 2097152 | tf_op jit(solution)/shard_map/final/pallas_call | solution.py:218
  (30 shorter events, 0.1 us)
Async XLA Ops:
  0.0 2.1 %collective-permute-start.4 = (bf16[64,4096]{1,0:T(8,128)(2,1)}, bf16[64,4096]{1,0:T(8,128)(2,1)S(1)}, u32[]{:S(2)}, u32[]{:S(2)}) collective-permute-start(bf16[64,4096]{1,0:T(8,128)(2,1)} %bitcast.10), channel_id=1, source_target_pairs={{0,1},{1,0},{2,3},{3,2},{4,5},{5,4},{6,7},{7,6},{8,9},{9,8},{10,11... | collective-permute-start | bytes 1572872 | tf_op jit(solution)/shard_map/ppermute | solution.py:28
  2.1 3.4 %copy-start = (bf16[64,256,256]{2,1,0:T(8,128)(2,1)S(1)}, bf16[64,256,256]{2,1,0:T(8,128)(2,1)}, u32[]{:S(2)}) copy-start(bf16[64,256,256]{2,1,0:T(8,128)(2,1)} %blocks.1) | copy-start | bytes 25165828
  5.5 1.0 %copy-start.2 = (bf16[4096,64]{0,1:T(8,128)(2,1)S(1)}, bf16[4096,64]{0,1:T(8,128)(2,1)}, u32[]{:S(2)}) copy-start(bf16[4096,64]{0,1:T(8,128)(2,1)} %param.19) | copy-start | bytes 1572868
  6.5 0.7 %copy-start.14 = (s32[64]{0:T(128)S(1)}, s32[64]{0:T(128)}, u32[]{:S(2)}) copy-start(s32[64]{0:T(128)} %row.3) | copy-start | bytes 772
  7.2 0.7 %copy-start.16 = (s32[64]{0:T(128)S(1)}, s32[64]{0:T(128)}, u32[]{:S(2)}) copy-start(s32[64]{0:T(128)} %col.1) | copy-start | bytes 772
  7.9 4.7 %copy-start.5 = (bf16[16,256,64]{1,2,0:T(8,128)(2,1)S(1)}, bf16[16,256,64]{1,2,0:T(8,128)(2,1)}, u32[]{:S(2)}) copy-start(bf16[16,256,64]{1,2,0:T(8,128)(2,1)} %param.23) | copy-start | bytes 1572868
  7.9 4.7 %copy-start.7 = (bf16[16,64,64]{2,1,0:T(8,128)(2,1)S(1)}, bf16[16,64,64]{2,1,0:T(8,128)(2,1)}, u32[]{:S(2)}) copy-start(bf16[16,64,64]{2,1,0:T(8,128)(2,1)} %param.25) | copy-start | bytes 393220
  7.9 4.7 %copy-start.10 = (bf16[8,64,64]{2,1,0:T(8,128)(2,1)S(1)}, bf16[8,64,64]{2,1,0:T(8,128)(2,1)}, u32[]{:S(2)}) copy-start(bf16[8,64,64]{2,1,0:T(8,128)(2,1)} %param.26) | copy-start | bytes 196612
  7.9 39.1 %copy-start.3 = (bf16[8,16,64,64]{3,2,1,0:T(8,128)(2,1)S(1)}, bf16[8,16,64,64]{3,2,1,0:T(8,128)(2,1)}, u32[]{:S(2)}) copy-start(bf16[8,16,64,64]{3,2,1,0:T(8,128)(2,1)} %param.30) | copy-start | bytes 3145732
  7.9 39.1 %copy-start.4 = (bf16[4,16,64,64]{3,2,1,0:T(8,128)(2,1)S(1)}, bf16[4,16,64,64]{3,2,1,0:T(8,128)(2,1)}, u32[]{:S(2)}) copy-start(bf16[4,16,64,64]{3,2,1,0:T(8,128)(2,1)} %param.31) | copy-start | bytes 1572868
  7.9 39.1 %copy-start.6 = (bf16[16,256,64]{1,2,0:T(8,128)(2,1)S(1)}, bf16[16,256,64]{1,2,0:T(8,128)(2,1)}, u32[]{:S(2)}) copy-start(bf16[16,256,64]{1,2,0:T(8,128)(2,1)} %param.24) | copy-start | bytes 1572868
  7.9 39.1 %copy-start.9 = (bf16[8,64,64]{2,1,0:T(8,128)(2,1)S(1)}, bf16[8,64,64]{2,1,0:T(8,128)(2,1)}, u32[]{:S(2)}) copy-start(bf16[8,64,64]{2,1,0:T(8,128)(2,1)} %spread_middle.1) | copy-start | bytes 196612
  12.2 34.8 %copy-start.1 = (bf16[16,16,64,64]{3,2,1,0:T(8,128)(2,1)S(1)}, bf16[16,16,64,64]{3,2,1,0:T(8,128)(2,1)}, u32[]{:S(2)}) copy-start(bf16[16,16,64,64]{3,2,1,0:T(8,128)(2,1)} %param.29) | copy-start | bytes 6291460
  12.3 34.8 %copy-start.8 = (bf16[16,64,64]{2,1,0:T(8,128)(2,1)S(1)}, bf16[16,64,64]{2,1,0:T(8,128)(2,1)}, u32[]{:S(2)}) copy-start(bf16[16,64,64]{2,1,0:T(8,128)(2,1)} %spread_leaf.1) | copy-start | bytes 393220
  12.3 34.8 %copy-start.11 = (s32[16,16]{1,0:T(8,128)S(1)}, s32[16,16]{1,0:T(8,128)}, u32[]{:S(2)}) copy-start(s32[16,16]{1,0:T(8,128)} %list_leaf.1) | copy-start | bytes 3076
  12.3 34.8 %copy-start.12 = (s32[8,16]{1,0:T(8,128)S(1)}, s32[8,16]{1,0:T(8,128)}, u32[]{:S(2)}) copy-start(s32[8,16]{1,0:T(8,128)} %list_middle.1) | copy-start | bytes 1540
  12.3 34.8 %copy-start.13 = (s32[4,16]{1,0:T(4,128)S(1)}, s32[4,16]{1,0:T(4,128)}, u32[]{:S(2)}) copy-start(s32[4,16]{1,0:T(4,128)} %list_top.1) | copy-start | bytes 772
  12.3 34.8 %copy-start.15 = (s32[64]{0:T(128)S(1)}, s32[64]{0:T(128)}, u32[]{:S(2)}) copy-start(s32[64]{0:T(128)} %row.3) | copy-start | bytes 772
  12.3 34.8 %copy-start.17 = (s32[16]{0:T(128)S(1)}, s32[16]{0:T(128)}, u32[]{:S(2)}) copy-start(s32[16]{0:T(128)} %count_leaf.1) | copy-start | bytes 196
  12.3 34.8 %copy-start.18 = (s32[8]{0:T(128)S(1)}, s32[8]{0:T(128)}, u32[]{:S(2)}) copy-start(s32[8]{0:T(128)} %count_middle.1) | copy-start | bytes 100
  12.3 34.8 %copy-start.19 = (s32[4]{0:T(128)S(1)}, s32[4]{0:T(128)}, u32[]{:S(2)}) copy-start(s32[4]{0:T(128)} %count_top.1) | copy-start | bytes 52
  12.3 11.1 %collective-permute-start.5 = (bf16[32,64,256]{2,1,0:T(8,128)(2,1)S(1)}, bf16[32,64,256]{2,1,0:T(8,128)(2,1)S(1)}, u32[]{:S(2)}, u32[]{:S(2)}) collective-permute-start(bf16[32,64,256]{2,1,0:T(8,128)(2,1)S(1)} %get-tuple-element.15), channel_id=1, source_target_pairs={{0,1},{1,0},{2,3},{3,2},{4,5},{5,4},{6,7},{7,6},{8,9},{9,8},{10,11... | collective-permute-start | bytes 3145736 | tf_op jit(solution)/shard_map/ppermute | solution.py:28
  14.6 16.6 %collective-permute-start.1 = (bf16[14,64,128]{2,1,0:T(8,128)(2,1)S(1)}, bf16[14,64,128]{2,1,0:T(8,128)(2,1)S(1)}, u32[]{:S(2)}, u32[]{:S(2)}) collective-permute-start(bf16[14,64,128]{2,1,0:T(8,128)(2,1)S(1)} %coeff.1.own.pack), channel_id=1, source_target_pairs={{0,126},{2,0},{4,2},{6,4},{8,6},{10,8},{12,10},{14,12},{16,14},{18... | collective-permute-start | bytes 688136 | tf_op jit(solution)/shard_map/ppermute | solution.py:24
  23.5 13.9 %collective-permute-start = (bf16[14,64,128]{2,1,0:T(8,128)(2,1)S(1)}, bf16[14,64,128]{2,1,0:T(8,128)(2,1)S(1)}, u32[]{:S(2)}, u32[]{:S(2)}) collective-permute-start(bf16[14,64,128]{2,1,0:T(8,128)(2,1)S(1)} %coeff.1.own.pack), channel_id=1, source_target_pairs={{0,2},{2,4},{4,6},{6,8},{8,10},{10,12},{12,14},{14,16},{16,18},{18... | collective-permute-start | bytes 688136 | tf_op jit(solution)/shard_map/ppermute | solution.py:24
  23.6 29.4 %collective-permute-start.6 = (bf16[8,64,256]{2,1,0:T(8,128)(2,1)S(1)}, bf16[8,64,256]{2,1,0:T(8,128)(2,1)S(1)}, u32[]{:S(2)}, u32[]{:S(2)}) collective-permute-start(bf16[8,64,256]{2,1,0:T(8,128)(2,1)S(1)} %get-tuple-element.17), channel_id=1, source_target_pairs={{0,2},{2,4},{4,6},{6,8},{8,10},{10,12},{12,14},{14,16},{16,18},{18... | collective-permute-start | bytes 786440 | tf_op jit(solution)/shard_map/ppermute | solution.py:24
  23.7 29.3 %collective-permute-start.7 = (bf16[8,64,256]{2,1,0:T(8,128)(2,1)S(1)}, bf16[8,64,256]{2,1,0:T(8,128)(2,1)S(1)}, u32[]{:S(2)}, u32[]{:S(2)}) collective-permute-start(bf16[8,64,256]{2,1,0:T(8,128)(2,1)S(1)} %get-tuple-element.18), channel_id=1, source_target_pairs={{0,126},{2,0},{4,2},{6,4},{8,6},{10,8},{12,10},{14,12},{16,14},{18... | collective-permute-start | bytes 786440 | tf_op jit(solution)/shard_map/ppermute | solution.py:24
  37.4 9.6 %collective-permute-start.2 = (bf16[10,64,128]{2,1,0:T(8,128)(2,1)S(1)}, bf16[10,64,128]{2,1,0:T(8,128)(2,1)S(1)}, u32[]{:S(2)}, u32[]{:S(2)}) collective-permute-start(bf16[10,64,128]{2,1,0:T(8,128)(2,1)S(1)} %get-tuple-element.12), channel_id=1, source_target_pairs={{0,6},{2,8},{4,10},{6,12},{8,14},{10,16},{12,18},{14,20},{16,22},{... | collective-permute-start | bytes 491528 | tf_op jit(solution)/shard_map/ppermute | solution.py:24
  37.5 9.5 %collective-permute-start.3 = (bf16[10,64,128]{2,1,0:T(8,128)(2,1)S(1)}, bf16[10,64,128]{2,1,0:T(8,128)(2,1)S(1)}, u32[]{:S(2)}, u32[]{:S(2)}) collective-permute-start(bf16[10,64,128]{2,1,0:T(8,128)(2,1)S(1)} %get-tuple-element.13), channel_id=1, source_target_pairs={{0,122},{2,124},{4,126},{6,0},{8,2},{10,4},{12,6},{14,8},{16,10},{... | collective-permute-start | bytes 491528 | tf_op jit(solution)/shard_map/ppermute | solution.py:24

commit v2 on v0

v2 whole, which is shorter than its diff:
```python
import jax
import jax.numpy as jnp
from jax import lax
from jax.experimental import pallas as pl
from jax.experimental.pallas import tpu as pltpu
from jax.sharding import PartitionSpec as P

F32 = jnp.float32
BF16 = jnp.bfloat16
VM = pl.BlockSpec(memory_space=pltpu.VMEM)
SM = pl.BlockSpec(memory_space=pltpu.SMEM)
HB = pl.BlockSpec(memory_space=pltpu.HBM)
AN = pl.BlockSpec(memory_space=pl.ANY)

N_PACK = 14
N_FAR_PACK = 10
CHUNKS = 8
FIRST = 16
TOP_AT = 40
ZERO_AT = TOP_AT + 36


def partners(count, distance, odd):
    partner = list(range(count))
    for i in range(odd, count - distance, 2):
        partner[i], partner[i + distance] = i + distance, i
    if distance == 3 and odd:
        for i, j in ((0, 2), (count - 3, count - 1)):
            partner[i], partner[j] = j, i
    return partner


def paired(block, distance, odd):
    partner = partners(lax.axis_size("leaf"), distance, odd)
    return lax.ppermute(block, "leaf", list(enumerate(partner)))


def swapped(block):
    return lax.ppermute(block, "rhs", [(0, 1), (1, 0)])


def in_hbm(array):
    return pltpu.with_memory_space_constraint(array, pltpu.HBM)


def mm(a, b):
    return lax.dot_general(a, b, (((1,), (0,)), ((), ())), preferred_element_type=F32)


def mm_t(a, b):
    return lax.dot_general(a, b, (((1,), (1,)), ((), ())), preferred_element_type=F32)


def started(*copies):
    made = [pltpu.make_async_copy(*c) for c in copies]
    for c in made:
        c.start()
    return made


def coeff_kernel(
    x_at, basis_at, lift_leaf_at, lift_middle_at, blocks, pack, x, held, basis, lift_leaf, lift_middle, sems
):
    copies = started(
        (x_at, x, sems.at[0]),
        (basis_at, basis, sems.at[1]),
        (lift_leaf_at, lift_leaf, sems.at[2]),
        (lift_middle_at, lift_middle, sems.at[3]),
        (blocks.at[pl.ds(0, FIRST)], held, sems.at[4]),
    )
    for c in copies[:4]:
        c.wait()
    for q in range(4):
        middles = []
        for p in (2 * q, 2 * q + 1):
            pair = [
                mm_t(x[:, l * 256 : (l + 1) * 256], basis[l]) for l in (2 * p, 2 * p + 1)
            ]
            block = jnp.concatenate(pair, axis=1).astype(BF16)
            pack[p] = block
            middles.append(mm(block, lift_leaf[p]))
        pack[8 + q] = jnp.concatenate(middles, axis=1).astype(BF16)
    for h in range(2):
        tops = [mm(pack[8 + q], lift_middle[q]) for q in (2 * h, 2 * h + 1)]
        pack[12 + h] = jnp.concatenate(tops, axis=1).astype(BF16)
    copies[4].wait()


def near_kernel(row_at, col_at, x, xp, held, blocks, acc, other, row, col, rest, sems):
    per = rest.shape[0] // CHUNKS
    places = started((row_at, row, sems.at[CHUNKS]), (col_at, col, sems.at[CHUNKS + 1]))
    copies = started(
        *[
            (blocks.at[pl.ds(FIRST + c * per, per)], rest.at[pl.ds(c * per, per)], sems.at[c])
            for c in range(CHUNKS)
        ]
    )
    acc[...] = jnp.zeros_like(acc)
    for c in places:
        c.wait()
    device = row[0] // 16
    for b in range(blocks.shape[0]):
        if b >= FIRST and (b - FIRST) % per == 0:
            copies[(b - FIRST) // per].wait()
        at = pl.multiple_of((row[b] - device * 16) * 256, 256)
        slot = col[b] - device * 16 + 8
        left = jnp.concatenate([x[:, pl.ds(at, 256)], xp[:, pl.ds(at, 256)]], axis=0)
        acc[slot] += mm(left, held[b] if b < FIRST else rest[b - FIRST])
    other[...] = acc[:, 64:].astype(BF16)


def pack_kernel(even, own, odd, carried, to_even, to_odd, carry):
    for out, near, far in ((to_even, even, odd), (to_odd, odd, even)):
        out[0:6] = near[8:14]
        out[6:8] = own[12:14]
        out[8:10] = far[12:14]


def place(row):
    device = row[0] // 16
    return device, 1 - 2 * (device % 2)


def first_lanes():
    return lax.broadcasted_iota(jnp.int32, (64, 128), 1) < 64


def double(dup, at, block):
    first = first_lanes()
    turned = jnp.concatenate([block[:, 64:], block[:, :64]], axis=1)
    dup[at] = jnp.where(first, block, turned)
    dup[at + 1] = jnp.where(first, turned, block)


def coupled(dup, zero_at, couple, lists, counts, t, base):
    live = counts[t]
    first = first_lanes()

    def source(j):
        return jnp.where(j < live, lists[t, j] + base, zero_at)

    gathered = jnp.concatenate(
        [jnp.where(first, dup[source(j)], dup[source(j + 1)]) for j in range(0, 16, 2)],
        axis=1,
    )
    return mm(gathered, couple[t])


def leaf_kernel(row, lists, counts, pack, even, odd, couple, far, dup):
    device, side = place(row)
    for i in range(8):
        for step, ref in ((0, pack), (side, even), (-side, odd)):
            double(dup, 16 * (1 + step) + 2 * i, ref[i])
    dup[48] = jnp.zeros((64, 128), BF16)
    for t in range(16):
        far[t] = coupled(dup, 48, couple, lists, counts, t, 16 - 16 * device)


def halo_kernel(row, acc, received, to_even, to_odd):
    device, side = place(row)
    for out, step in ((to_even, side), (to_odd, -side)):
        at = 12 + 12 * step
        out[...] = (acc[pl.ds(at, 8), :64] + received[pl.ds(at, 8)].astype(F32)).astype(BF16)


def tops_kernel(
    row,
    list_middle,
    list_top,
    count_middle,
    count_top,
    pack,
    even,
    odd,
    far_even,
    far_odd,
    couple_middle,
    couple_top,
    spread_middle,
    after,
    down_middle,
    dup,
):
    device, side = place(row)
    held = [(pack, 0, 8, 12)]
    for sign, beside, away in ((side, even, far_even), (-side, odd, far_odd)):
        held += [
            (beside, sign, 8, 12),
            (away, 2 * sign, 0, 4),
            (away, 3 * sign, None, 6),
            (away, 4 * sign, None, 8),
        ]
    for ref, step, middle_at, top_at in held:
        for i in range(2):
            double(dup, TOP_AT + 4 * (4 + step) + 2 * i, ref[top_at + i])
        if middle_at is not None:
            for i in range(4):
                double(dup, 8 * (2 + step) + 2 * i, ref[middle_at + i])
    dup[ZERO_AT] = jnp.zeros((64, 128), BF16)
    down_top = [
        coupled(
            dup, ZERO_AT, couple_top, list_top, count_top, t, TOP_AT + 16 - 4 * device
        ).astype(BF16)
        for t in range(4)
    ]
    for t in range(8):
        down_middle[t] = (
            coupled(dup, ZERO_AT, couple_middle, list_middle, count_middle, t, 16 - 8 * device)
            + mm_t(down_top[t // 2], spread_middle[t])
        ).astype(BF16)


def finish_kernel(far, down_middle, spread_leaf, bases, acc, received, out):
    for t in range(16):
        down = (far[t] + mm_t(down_middle[t // 2], spread_leaf[t])).astype(BF16)
        out[t] = mm(down, bases[t]) + (acc[8 + t, :64] + received[8 + t].astype(F32))


def final_kernel(row, total, from_even, from_odd, out):
    device, side = place(row)
    for halo, step in ((from_even, side), (from_odd, -side)):
        for k in range(8):
            l = 4 + 4 * step + k
            at = pl.multiple_of(l * 256, 256)
            out[:, pl.ds(at, 256)] = (total[l] + halo[k].astype(F32)).astype(BF16)


def shaped(*shape, dtype=BF16):
    return jax.ShapeDtypeStruct(shape, dtype)


def call(name, kernel, ins, outs, *args, scratch=(), alias=None, mib=8, work=0):
    specs = {"v": VM, "s": SM, "h": HB, "a": AN}
    kinds, made = ins.split(">")
    return pl.pallas_call(
        kernel,
        name=name,
        in_specs=[specs[k] for k in kinds],
        out_shape=outs,
        out_specs=[specs[k] for k in made],
        scratch_shapes=scratch,
        input_output_aliases=alias or {},
        compiler_params=pltpu.CompilerParams(vmem_limit_bytes=mib << 20),
        cost_estimate=pl.CostEstimate(flops=work, bytes_accessed=work // 300, transcendentals=0),
    )(*args)


def shards(
    operand,
    near_blocks,
    near_row,
    near_column,
    row_basis,
    leaf_column_bases,
    lift_leaf,
    lift_middle,
    spread_middle,
    spread_leaf,
    couple_leaf,
    couple_middle,
    couple_top,
    list_leaf,
    list_middle,
    list_top,
    count_leaf,
    count_middle,
    count_top,
):
    x = operand.T
    xp = swapped(x)
    blocks = in_hbm(near_blocks)
    pack, x_held, held = call(
        "coeff",
        coeff_kernel,
        "hhhhh>vvv",
        [shaped(N_PACK, 64, 128), shaped(64, 4096), shaped(FIRST, 256, 256)],
        in_hbm(x),
        in_hbm(jnp.swapaxes(row_basis, 1, 2)),
        in_hbm(lift_leaf.reshape(8, 128, 64)),
        in_hbm(lift_middle.reshape(4, 128, 64)),
        blocks,
        scratch=[
            pltpu.VMEM((16, 64, 256), BF16),
            pltpu.VMEM((8, 128, 64), BF16),
            pltpu.VMEM((4, 128, 64), BF16),
            pltpu.SemaphoreType.DMA((5,)),
        ],
    )
    even, odd = paired(pack, 1, 0), paired(pack, 1, 1)
    acc, other = call(
        "near",
        near_kernel,
        "hhvvvh>vv",
        [shaped(32, 128, 256, dtype=F32), shaped(32, 64, 256)],
        in_hbm(near_row),
        in_hbm(near_column),
        x_held,
        xp,
        held,
        blocks,
        scratch=[
            pltpu.SMEM((64,), jnp.int32),
            pltpu.SMEM((64,), jnp.int32),
            pltpu.VMEM((64 - FIRST, 256, 256), BF16),
            pltpu.SemaphoreType.DMA((CHUNKS + 2,)),
        ],
        mib=16,
        work=23000000000,
    )
    far_pack = shaped(N_FAR_PACK, 64, 128)
    to_even, to_odd, other = call(
        "pack",
        pack_kernel,
        "vvva>vva",
        [far_pack, far_pack, shaped(32, 64, 256)],
        even,
        pack,
        odd,
        other,
        alias={3: 2},
    )
    received = swapped(other)
    far_even, far_odd = paired(to_even, 3, 0), paired(to_odd, 3, 1)
    halos = shaped(8, 64, 256)
    [far] = call(
        "leaf",
        leaf_kernel,
        "sssvvvv>v",
        [shaped(16, 64, 64, dtype=F32)],
        near_row,
        list_leaf,
        count_leaf,
        pack,
        even,
        odd,
        couple_leaf.reshape(16, 1024, 64),
        scratch=[pltpu.VMEM((49, 64, 128), BF16)],
        work=23000000000,
    )
    halo_even, halo_odd = call(
        "halo",
        halo_kernel,
        "svv>vv",
        [halos] * 2,
        near_row,
        acc,
        received,
    )
    from_even, from_odd = paired(halo_even, 1, 0), paired(halo_odd, 1, 1)
    [down_middle] = call(
        "tops",
        tops_kernel,
        "sssssvvvvvvvva>v",
        [shaped(8, 64, 64)],
        near_row,
        list_middle,
        list_top,
        count_middle,
        count_top,
        pack,
        even,
        odd,
        far_even,
        far_odd,
        couple_middle.reshape(8, 1024, 64),
        couple_top.reshape(4, 1024, 64),
        spread_middle,
        far,
        scratch=[pltpu.VMEM((ZERO_AT + 1, 64, 128), BF16)],
        work=1150000000,
    )
    [total] = call(
        "finish",
        finish_kernel,
        "vvvvvv>v",
        [shaped(16, 64, 256, dtype=F32)],
        far,
        down_middle,
        spread_leaf,
        jnp.swapaxes(leaf_column_bases, 1, 2),
        acc,
        received,
        work=1150000000,
    )
    [out] = call(
        "final",
        final_kernel,
        "svvv>v",
        [shaped(64, 4096)],
        near_row,
        total,
        from_even,
        from_odd,
    )
    return out.T


def solution(mesh):
    return jax.shard_map(
        shards,
        mesh=mesh,
        in_specs=(
            P("leaf", "rhs"),
            P(("leaf", "rhs"), None, None),
            P(("leaf", "rhs")),
            P(("leaf", "rhs")),
            P("leaf", None, None),
            P("leaf", None, None),
            P("leaf", None, None),
            P("leaf", None, None),
            P("leaf", None, None),
            P("leaf", None, None),
            P("leaf", None, None, None),
            P("leaf", None, None, None),
            P("leaf", None, None, None),
            P("leaf", None),
            P("leaf", None),
            P("leaf", None),
            P("leaf"),
            P("leaf"),
            P("leaf"),
        ),
        out_specs=P("leaf", "rhs"),
        check_vma=False,
    )
```

time: 172 us -> 41 us (0.24)
  starting transfers between devices: 66.9 us -> 18 us
  local copies, waits for them, and re-layouts: 30.9 us -> 0.08 us
  matrix products: 28.1 us -> 0 us
  other arithmetic: 24.4 us -> 0 us
  Pallas kernels: 0 us -> 15.1 us
  between operations: 14.5 us -> 0.32 us
  waiting for transfers between devices: 3.81 us -> 7.31 us
  blocking collectives: 1.82 us -> 0 us
    ppermute x16 -> x8, starting transfers between devices: 66.8 us -> 18 us  [the longest x6 18 us: paired(): return lax.ppermute(block, 'leaf', list(enumerate(partner)))]
    dot_general x10 -> x0, matrix products: 28.1 us -> none  [the longest x1 13.4 us: near_terms(): jnp.einsum('bij,bir->bjr', blocks, picked, preferred_element_type=jnp.flo...]
    scatter-add x1 -> x0, other arithmetic: 17.1 us -> none  [near_terms(): jax.ops.segment_sum(products, slots, num_segments=leaf_clusters + 2 * mar...]
    gather x5 -> x0, local copies, waits for them, and re-layouts: 16.2 us -> none  [the longest x4 13.4 us: couple_level(): picked = jnp.take(coeffs, (sources - lowest).reshape(-1), axis=0)]
    pallas_call x0 -> x8, Pallas kernels: none -> 15.1 us  [call(): pl.pallas_call(kernel, name=name, in_specs=[specs[k] for k in kinds], out...]
    unnamed x57 -> x26, local copies, waits for them, and re-layouts: 12.3 us -> 0.08 us
    ppermute x16 -> x8, waiting for transfers between devices: 3.13 us -> 7.31 us  [the longest x6 7.3 us: paired(): return lax.ppermute(block, 'leaf', list(enumerate(partner)))]
    lt x2 -> x0, other arithmetic: 2.5 us -> none  [couple_level(): live_slot = jnp.arange(sources.shape[1])[None, :] < entry_counts[:, None]]
  transfers between devices with their start and end apart: 17 -> 8, of which waited for: 1 -> 2; matrix products, arithmetic and copies ran while one was open for 28% -> 0% of each run, Pallas kernels for 0% -> 33%
where the time goes in v2:
time: 41 us; the launch traced here: 40.9 us
  starting transfers between devices  18 us (44%)
  Pallas kernels  15.1 us (37%)
  waiting for transfers between devices  7.31 us (18%)
    ppermute x6, starting transfers between devices, paired(): return lax.ppermute(block, 'leaf', list(enumerate(partner)))  18 us
    pallas_call x8, Pallas kernels, call(): pl.pallas_call(kernel, name=name, in_specs=[specs[k] for k in kinds], out...  15.1 us
    ppermute x6, waiting for transfers between devices, paired(): return lax.ppermute(block, 'leaf', list(enumerate(partner)))  7.3 us
  transfers between devices with their start and end apart: 8, of which 2 were waited for; matrix products, arithmetic and copies ran while one was open for 0% of the time, Pallas kernels for 33%

profile of v2, /device:TPU:16, one launch (start us, length us, event | category | flops | bytes accessed | tf_op | source)
XLA Modules:
  0.0 40.9 jit_solution(3832255146470320810)
XLA Ops:
  0.0 0.0 collective-permute-start.2
  0.0 3.4 %coeff.1 = (bf16[14,64,128]{2,1,0:T(8,128)(2,1)S(1)}, bf16[64,4096]{1,0:T(8,128)(2,1)S(1)}, bf16[16,256,256]{2,1,0:T(8,128)(2,1)S(1)}) custom-call(bf16[64,4096]{1,0:T(8,128)(2,1)} %bitcast.15, bf16[16,64,256]{2,1,0:T(8,128)(2,1)} %bitcast.13, bf16[8,128,64]{2,1,0:T(8,128)(2,1)} %bitcast.16, bf16[4,128,64]{2,1,0:T(8,128)(2,1)} %bitcast.17, ...), custom_call_target="tpu_custom_call" | custom-call | tf_op jit(solution)/shard_map/coeff/pallas_call | solution.py:235
  3.4 2.0 %collective-permute-start = (bf16[14,64,128]{2,1,0:T(8,128)(2,1)S(1)}, bf16[14,64,128]{2,1,0:T(8,128)(2,1)S(1)}, u32[]{:S(2)}, u32[]{:S(2)}) collective-permute-start(bf16[14,64,128]{2,1,0:T(8,128)(2,1)S(1)} %get-tuple-element.15.pack.own), channel_id=1, source_target_pairs={{0,2},{2,0},{4,6},{6,4},{8,10},{10,8},{12,14},{14,12},{16,18},{18,... | collective-permute-start | bytes 688136 | tf_op jit(solution)/shard_map/ppermute | solution.py:35
  5.4 6.5 %collective-permute-start.1 = (bf16[14,64,128]{2,1,0:T(8,128)(2,1)S(1)}, bf16[14,64,128]{2,1,0:T(8,128)(2,1)S(1)}, u32[]{:S(2)}, u32[]{:S(2)}) collective-permute-start(bf16[14,64,128]{2,1,0:T(8,128)(2,1)S(1)} %get-tuple-element.15.pack.own), channel_id=1, source_target_pairs={{0,0},{2,4},{4,2},{6,8},{8,6},{10,12},{12,10},{14,16},{16,14},{18,... | collective-permute-start | bytes 688136 | tf_op jit(solution)/shard_map/ppermute | solution.py:35
  11.9 0.0 copy-start.5
  11.9 3.9 %near.1 = (f32[32,128,256]{2,1,0:T(8,128)S(1)}, bf16[32,64,256]{2,1,0:T(8,128)(2,1)S(1)}) custom-call(s32[64]{0:T(128)} %row.7, s32[64]{0:T(128)} %col_at.1, bf16[64,4096]{1,0:T(8,128)(2,1)S(1)} %get-tuple-element.16.x, bf16[64,4096]{1,0:T(8,128)(2,1)S(1)} %collective-permute-done.2.xp, bf16[16,256,256]{2,1,0:T(8,128)(2,1)S(1)} %get-tuple-element.17.held, ...), custom_call_target="tpu_custom_call" | custom-call | flops 23000000512 | bytes 76666664 | tf_op jit(solution)/shard_map/near/pallas_call | solution.py:235
  15.8 0.0 copy-start.10
  15.8 0.0 copy-start.11
  15.9 0.0 copy-start.12
  15.9 0.0 collective-permute-done.even
  15.9 3.4 %collective-permute-done.1.odd = bf16[14,64,128]{2,1,0:T(8,128)(2,1)S(1)} collective-permute-done((bf16[14,64,128]{2,1,0:T(8,128)(2,1)S(1)}, bf16[14,64,128]{2,1,0:T(8,128)(2,1)S(1)}, u32[]{:S(2)}, u32[]{:S(2)}) %collective-permute-start.1) | collective-permute-done | bytes 229408 | tf_op jit(solution)/shard_map/ppermute | solution.py:35
  19.3 0.1 collective-permute-start.5
  19.4 2.3 %collective-permute-start.3 = (bf16[10,64,128]{2,1,0:T(8,128)(2,1)S(1)}, bf16[10,64,128]{2,1,0:T(8,128)(2,1)S(1)}, u32[]{:S(2)}, u32[]{:S(2)}) collective-permute-start(bf16[10,64,128]{2,1,0:T(8,128)(2,1)S(1)} %get-tuple-element.19), channel_id=1, source_target_pairs={{0,6},{2,2},{4,10},{6,0},{8,14},{10,4},{12,18},{14,8},{16,22},{18,... | collective-permute-start | bytes 491528 | tf_op jit(solution)/shard_map/ppermute | solution.py:35
  21.7 1.3 %collective-permute-start.4 = (bf16[10,64,128]{2,1,0:T(8,128)(2,1)S(1)}, bf16[10,64,128]{2,1,0:T(8,128)(2,1)S(1)}, u32[]{:S(2)}, u32[]{:S(2)}) collective-permute-start(bf16[10,64,128]{2,1,0:T(8,128)(2,1)S(1)} %get-tuple-element.20), channel_id=1, source_target_pairs={{0,4},{2,8},{4,0},{6,12},{8,2},{10,16},{12,6},{14,20},{16,10},{18,... | collective-permute-start | bytes 491528 | tf_op jit(solution)/shard_map/ppermute | solution.py:35
  23.0 0.6 %halo.1 = (bf16[8,64,256]{2,1,0:T(8,128)(2,1)S(1)}, bf16[8,64,256]{2,1,0:T(8,128)(2,1)S(1)}) custom-call(s32[64]{0:T(128)S(1)} %copy-done.5, f32[32,128,256]{2,1,0:T(8,128)S(1)} %get-tuple-element.21.acc, bf16[32,64,256]{2,1,0:T(8,128)(2,1)S(1)} %collective-permute-done.5.received), custom_call_target="tpu_custom_call" | custom-call | tf_op jit(solution)/shard_map/halo/pallas_call | solution.py:235
  23.7 1.8 %collective-permute-start.6 = (bf16[8,64,256]{2,1,0:T(8,128)(2,1)S(1)}, bf16[8,64,256]{2,1,0:T(8,128)(2,1)S(1)}, u32[]{:S(2)}, u32[]{:S(2)}) collective-permute-start(bf16[8,64,256]{2,1,0:T(8,128)(2,1)S(1)} %get-tuple-element.23), channel_id=1, source_target_pairs={{0,2},{2,0},{4,6},{6,4},{8,10},{10,8},{12,14},{14,12},{16,18},{18,... | collective-permute-start | bytes 786440 | tf_op jit(solution)/shard_map/ppermute | solution.py:35
  25.5 4.0 %collective-permute-start.7 = (bf16[8,64,256]{2,1,0:T(8,128)(2,1)S(1)}, bf16[8,64,256]{2,1,0:T(8,128)(2,1)S(1)}, u32[]{:S(2)}, u32[]{:S(2)}) collective-permute-start(bf16[8,64,256]{2,1,0:T(8,128)(2,1)S(1)} %get-tuple-element.24), channel_id=1, source_target_pairs={{0,0},{2,4},{4,2},{6,8},{8,6},{10,12},{12,10},{14,16},{16,14},{18,... | collective-permute-start | bytes 786440 | tf_op jit(solution)/shard_map/ppermute | solution.py:35
  29.5 0.0 copy-start
  29.6 0.0 copy-start.1
  29.6 0.0 copy-start.4
  29.6 0.0 copy-start.6
  29.6 0.0 copy-start.7
  29.6 0.0 copy-start.8
  29.6 0.0 copy-start.9
  29.6 1.8 %leaf.1.after.far = f32[16,64,64]{2,1,0:T(8,128)S(1)} custom-call(s32[64]{0:T(128)S(1)} %copy-done.5, s32[16,16]{1,0:T(8,128)S(1)} %copy-done.11, s32[16]{0:T(128)S(1)} %copy-done.12, bf16[14,64,128]{2,1,0:T(8,128)(2,1)S(1)} %get-tuple-element.15.pack.own, bf16[14,64,128]{2,1,0:T(8,128)(2,1)S(1)} %collective-permute-done.even, ...), custom_call_target="tpu_custom_call" | custom-call | flops 23000000512 | bytes 76666664 | tf_op jit(solution)/shard_map/leaf/pallas_call | solution.py:235
  31.4 0.0 copy-start.2
  31.4 0.0 copy-start.3
  31.4 0.0 collective-permute-done.4.far_odd
  31.5 1.6 %tops.1.down_middle = bf16[8,64,64]{2,1,0:T(8,128)(2,1)S(1)} custom-call(s32[64]{0:T(128)S(1)} %copy-done.5, s32[8,16]{1,0:T(8,128)S(1)} %copy-done.6, s32[4,16]{1,0:T(4,128)S(1)} %copy-done.7, s32[8]{0:T(128)S(1)} %copy-done.8, s32[4]{0:T(128)S(1)} %copy-done.9, bf16[14,64,128]{2,1,0:T(8,128)(2,1)S(1)} %get-tuple-element.15.pack.own, ...), custom_call_target="tpu_custom_call" | custom-call | flops 1150000000 | bytes 3833333 | tf_op jit(solution)/shard_map/tops/pallas_call | solution.py:235
  33.2 2.3 %finish.1.total = f32[16,64,256]{2,1,0:T(8,128)S(1)} custom-call(f32[16,64,64]{2,1,0:T(8,128)S(1)} %leaf.1.after.far, bf16[8,64,64]{2,1,0:T(8,128)(2,1)S(1)} %tops.1.down_middle, bf16[16,64,64]{2,1,0:T(8,128)(2,1)S(1)} %copy-done.3, bf16[16,64,256]{2,1,0:T(8,128)(2,1)S(1)} %bitcast.11, f32[32,128,256]{2,1,0:T(8,128)S(1)} %get-tuple-element.21.acc, ...), custom_call_target="tpu_custom_call" | custom-call | flops 1150000000 | bytes 3833333 | tf_op jit(solution)/shard_map/finish/pallas_call | solution.py:235
  35.5 3.9 %collective-permute-done.7.from_odd = bf16[8,64,256]{2,1,0:T(8,128)(2,1)S(1)} collective-permute-done((bf16[8,64,256]{2,1,0:T(8,128)(2,1)S(1)}, bf16[8,64,256]{2,1,0:T(8,128)(2,1)S(1)}, u32[]{:S(2)}, u32[]{:S(2)}) %collective-permute-start.7) | collective-permute-done | bytes 262176 | tf_op jit(solution)/shard_map/ppermute | solution.py:35
  39.4 1.5 %final.1 = bf16[64,4096]{1,0:T(8,128)(2,1)} custom-call(s32[64]{0:T(128)S(1)} %copy-done.5, f32[16,64,256]{2,1,0:T(8,128)S(1)} %finish.1.total, bf16[8,64,256]{2,1,0:T(8,128)(2,1)S(1)} %collective-permute-done.6.from_even, bf16[8,64,256]{2,1,0:T(8,128)(2,1)S(1)} %collective-permute-done.7.from_odd), custom_call_target="tpu_custom_call" | custom-call | tf_op jit(solution)/shard_map/final/pallas_call | solution.py:235
  (18 shorter events, 0.1 us)
Async XLA Ops:
  0.0 11.9 %collective-permute-start.2 = (bf16[64,4096]{1,0:T(8,128)(2,1)}, bf16[64,4096]{1,0:T(8,128)(2,1)S(1)}, u32[]{:S(2)}, u32[]{:S(2)}) collective-permute-start(bf16[64,4096]{1,0:T(8,128)(2,1)} %bitcast.14), channel_id=1, source_target_pairs={{0,1},{1,0},{2,3},{3,2},{4,5},{5,4},{6,7},{7,6},{8,9},{9,8},{10,11... | collective-permute-start | bytes 1572872 | tf_op jit(solution)/shard_map/ppermute | solution.py:39
  3.4 12.5 %collective-permute-start = (bf16[14,64,128]{2,1,0:T(8,128)(2,1)S(1)}, bf16[14,64,128]{2,1,0:T(8,128)(2,1)S(1)}, u32[]{:S(2)}, u32[]{:S(2)}) collective-permute-start(bf16[14,64,128]{2,1,0:T(8,128)(2,1)S(1)} %get-tuple-element.15.pack.own), channel_id=1, source_target_pairs={{0,2},{2,0},{4,6},{6,4},{8,10},{10,8},{12,14},{14,12},{16,18},{18,... | collective-permute-start | bytes 688136 | tf_op jit(solution)/shard_map/ppermute | solution.py:35
  5.4 13.8 %collective-permute-start.1 = (bf16[14,64,128]{2,1,0:T(8,128)(2,1)S(1)}, bf16[14,64,128]{2,1,0:T(8,128)(2,1)S(1)}, u32[]{:S(2)}, u32[]{:S(2)}) collective-permute-start(bf16[14,64,128]{2,1,0:T(8,128)(2,1)S(1)} %get-tuple-element.15.pack.own), channel_id=1, source_target_pairs={{0,0},{2,4},{4,2},{6,8},{8,6},{10,12},{12,10},{14,16},{16,14},{18,... | collective-permute-start | bytes 688136 | tf_op jit(solution)/shard_map/ppermute | solution.py:35
  11.9 11.1 %copy-start.5 = (s32[64]{0:T(128)S(1)}, s32[64]{0:T(128)}, u32[]{:S(2)}) copy-start(s32[64]{0:T(128)} %row.7) | copy-start | bytes 772
  15.8 13.7 %copy-start.10 = (bf16[16,16,64,64]{3,2,1,0:T(8,128)(2,1)S(1)}, bf16[16,16,64,64]{3,2,1,0:T(8,128)(2,1)}, u32[]{:S(2)}) copy-start(bf16[16,16,64,64]{3,2,1,0:T(8,128)(2,1)} %param.29) | copy-start | bytes 6291460
  15.8 13.7 %copy-start.11 = (s32[16,16]{1,0:T(8,128)S(1)}, s32[16,16]{1,0:T(8,128)}, u32[]{:S(2)}) copy-start(s32[16,16]{1,0:T(8,128)} %lists.1) | copy-start | bytes 3076
  15.9 13.7 %copy-start.12 = (s32[16]{0:T(128)S(1)}, s32[16]{0:T(128)}, u32[]{:S(2)}) copy-start(s32[16]{0:T(128)} %counts.1) | copy-start | bytes 196
  19.3 3.8 %collective-permute-start.5 = (bf16[32,64,256]{2,1,0:T(8,128)(2,1)S(1)}, bf16[32,64,256]{2,1,0:T(8,128)(2,1)S(1)}, u32[]{:S(2)}, u32[]{:S(2)}) collective-permute-start(bf16[32,64,256]{2,1,0:T(8,128)(2,1)S(1)} %get-tuple-element.22), channel_id=1, source_target_pairs={{0,1},{1,0},{2,3},{3,2},{4,5},{5,4},{6,7},{7,6},{8,9},{9,8},{10,11... | collective-permute-start | bytes 3145736 | tf_op jit(solution)/shard_map/ppermute | solution.py:39
  19.4 12.1 %collective-permute-start.3 = (bf16[10,64,128]{2,1,0:T(8,128)(2,1)S(1)}, bf16[10,64,128]{2,1,0:T(8,128)(2,1)S(1)}, u32[]{:S(2)}, u32[]{:S(2)}) collective-permute-start(bf16[10,64,128]{2,1,0:T(8,128)(2,1)S(1)} %get-tuple-element.19), channel_id=1, source_target_pairs={{0,6},{2,2},{4,10},{6,0},{8,14},{10,4},{12,18},{14,8},{16,22},{18,... | collective-permute-start | bytes 491528 | tf_op jit(solution)/shard_map/ppermute | solution.py:35
  21.7 9.7 %collective-permute-start.4 = (bf16[10,64,128]{2,1,0:T(8,128)(2,1)S(1)}, bf16[10,64,128]{2,1,0:T(8,128)(2,1)S(1)}, u32[]{:S(2)}, u32[]{:S(2)}) collective-permute-start(bf16[10,64,128]{2,1,0:T(8,128)(2,1)S(1)} %get-tuple-element.20), channel_id=1, source_target_pairs={{0,4},{2,8},{4,0},{6,12},{8,2},{10,16},{12,6},{14,20},{16,10},{18,... | collective-permute-start | bytes 491528 | tf_op jit(solution)/shard_map/ppermute | solution.py:35
  23.7 11.8 %collective-permute-start.6 = (bf16[8,64,256]{2,1,0:T(8,128)(2,1)S(1)}, bf16[8,64,256]{2,1,0:T(8,128)(2,1)S(1)}, u32[]{:S(2)}, u32[]{:S(2)}) collective-permute-start(bf16[8,64,256]{2,1,0:T(8,128)(2,1)S(1)} %get-tuple-element.23), channel_id=1, source_target_pairs={{0,2},{2,0},{4,6},{6,4},{8,10},{10,8},{12,14},{14,12},{16,18},{18,... | collective-permute-start | bytes 786440 | tf_op jit(solution)/shard_map/ppermute | solution.py:35
  25.5 14.0 %collective-permute-start.7 = (bf16[8,64,256]{2,1,0:T(8,128)(2,1)S(1)}, bf16[8,64,256]{2,1,0:T(8,128)(2,1)S(1)}, u32[]{:S(2)}, u32[]{:S(2)}) collective-permute-start(bf16[8,64,256]{2,1,0:T(8,128)(2,1)S(1)} %get-tuple-element.24), channel_id=1, source_target_pairs={{0,0},{2,4},{4,2},{6,8},{8,6},{10,12},{12,10},{14,16},{16,14},{18,... | collective-permute-start | bytes 786440 | tf_op jit(solution)/shard_map/ppermute | solution.py:35
  29.5 1.9 %copy-start = (bf16[8,16,64,64]{3,2,1,0:T(8,128)(2,1)S(1)}, bf16[8,16,64,64]{3,2,1,0:T(8,128)(2,1)}, u32[]{:S(2)}) copy-start(bf16[8,16,64,64]{3,2,1,0:T(8,128)(2,1)} %param.30) | copy-start | bytes 3145732
  29.6 1.9 %copy-start.1 = (bf16[4,16,64,64]{3,2,1,0:T(8,128)(2,1)S(1)}, bf16[4,16,64,64]{3,2,1,0:T(8,128)(2,1)}, u32[]{:S(2)}) copy-start(bf16[4,16,64,64]{3,2,1,0:T(8,128)(2,1)} %param.31) | copy-start | bytes 1572868
  29.6 1.9 %copy-start.4 = (bf16[8,64,64]{2,1,0:T(8,128)(2,1)S(1)}, bf16[8,64,64]{2,1,0:T(8,128)(2,1)}, u32[]{:S(2)}) copy-start(bf16[8,64,64]{2,1,0:T(8,128)(2,1)} %spread_middle.1) | copy-start | bytes 196612
  29.6 1.9 %copy-start.6 = (s32[8,16]{1,0:T(8,128)S(1)}, s32[8,16]{1,0:T(8,128)}, u32[]{:S(2)}) copy-start(s32[8,16]{1,0:T(8,128)} %list_middle.1) | copy-start | bytes 1540
  29.6 1.9 %copy-start.7 = (s32[4,16]{1,0:T(4,128)S(1)}, s32[4,16]{1,0:T(4,128)}, u32[]{:S(2)}) copy-start(s32[4,16]{1,0:T(4,128)} %list_top.1) | copy-start | bytes 772
  29.6 1.9 %copy-start.8 = (s32[8]{0:T(128)S(1)}, s32[8]{0:T(128)}, u32[]{:S(2)}) copy-start(s32[8]{0:T(128)} %count_middle.1) | copy-start | bytes 100
  29.6 1.9 %copy-start.9 = (s32[4]{0:T(128)S(1)}, s32[4]{0:T(128)}, u32[]{:S(2)}) copy-start(s32[4]{0:T(128)} %count_top.1) | copy-start | bytes 52
  31.4 1.8 %copy-start.2 = (bf16[16,256,64]{1,2,0:T(8,128)(2,1)S(1)}, bf16[16,256,64]{1,2,0:T(8,128)(2,1)}, u32[]{:S(2)}) copy-start(bf16[16,256,64]{1,2,0:T(8,128)(2,1)} %param.24) | copy-start | bytes 1572868
  31.4 1.8 %copy-start.3 = (bf16[16,64,64]{2,1,0:T(8,128)(2,1)S(1)}, bf16[16,64,64]{2,1,0:T(8,128)(2,1)}, u32[]{:S(2)}) copy-start(bf16[16,64,64]{2,1,0:T(8,128)(2,1)} %spread_leaf.1) | copy-start | bytes 393220

commit v3 on v2

--- a/solution.py
+++ b/solution.py
@@ -21,18 +21,25 @@
 
 
 def partners(count, distance, odd):
-    partner = list(range(count))
+    partner = {(i, c): (i, 1 - c) for i in range(count) for c in (0, 1)}
+
+    def pair(i, j, crossed):
+        for c in (0, 1):
+            partner[i, c], partner[j, c ^ crossed] = (j, c ^ crossed), (i, c)
+
     for i in range(odd, count - distance, 2):
-        partner[i], partner[i + distance] = i + distance, i
+        pair(i, i + distance, 0)
     if distance == 3 and odd:
-        for i, j in ((0, 2), (count - 3, count - 1)):
-            partner[i], partner[j] = j, i
+        pair(0, 2, 1)
+        pair(count - 3, count - 1, 1)
     return partner
 
 
 def paired(block, distance, odd):
     partner = partners(lax.axis_size("leaf"), distance, odd)
-    return lax.ppermute(block, "leaf", list(enumerate(partner)))
+    cores = lax.axis_size("rhs")
+    route = [(i * cores + c, j * cores + d) for (i, c), (j, d) in sorted(partner.items())]
+    return lax.ppermute(block, ("leaf", "rhs"), route)
 
 
 def swapped(block):
@@ -98,7 +105,7 @@
     acc[...] = jnp.zeros_like(acc)
     for c in places:
         c.wait()
-    device = row[0] // 16
+    device, _ = place()
     for b in range(blocks.shape[0]):
         if b >= FIRST and (b - FIRST) % per == 0:
             copies[(b - FIRST) // per].wait()
@@ -109,15 +116,15 @@
     other[...] = acc[:, 64:].astype(BF16)
 
 
-def pack_kernel(even, own, odd, carried, to_even, to_odd, carry):
+def pack_kernel(even, own, odd, to_even, to_odd):
     for out, near, far in ((to_even, even, odd), (to_odd, odd, even)):
         out[0:6] = near[8:14]
         out[6:8] = own[12:14]
         out[8:10] = far[12:14]
 
 
-def place(row):
-    device = row[0] // 16
+def place():
+    device = lax.axis_index("leaf")
     return device, 1 - 2 * (device % 2)
 
 
@@ -146,8 +153,8 @@
     return mm(gathered, couple[t])
 
 
-def leaf_kernel(row, lists, counts, pack, even, odd, couple, far, dup):
-    device, side = place(row)
+def leaf_kernel(lists, counts, pack, even, odd, couple, far, dup):
+    device, side = place()
     for i in range(8):
         for step, ref in ((0, pack), (side, even), (-side, odd)):
             double(dup, 16 * (1 + step) + 2 * i, ref[i])
@@ -156,15 +163,14 @@
         far[t] = coupled(dup, 48, couple, lists, counts, t, 16 - 16 * device)
 
 
-def halo_kernel(row, acc, received, to_even, to_odd):
-    device, side = place(row)
+def halo_kernel(acc, received, to_even, to_odd):
+    device, side = place()
     for out, step in ((to_even, side), (to_odd, -side)):
         at = 12 + 12 * step
         out[...] = (acc[pl.ds(at, 8), :64] + received[pl.ds(at, 8)].astype(F32)).astype(BF16)
 
 
 def tops_kernel(
-    row,
     list_middle,
     list_top,
     count_middle,
@@ -181,7 +187,7 @@
     down_middle,
     dup,
 ):
-    device, side = place(row)
+    device, side = place()
     held = [(pack, 0, 8, 12)]
     for sign, beside, away in ((side, even, far_even), (-side, odd, far_odd)):
         held += [
@@ -216,8 +222,8 @@
         out[t] = mm(down, bases[t]) + (acc[8 + t, :64] + received[8 + t].astype(F32))
 
 
-def final_kernel(row, total, from_even, from_odd, out):
-    device, side = place(row)
+def final_kernel(total, from_even, from_odd, out):
+    device, side = place()
     for halo, step in ((from_even, side), (from_odd, -side)):
         for k in range(8):
             l = 4 + 4 * step + k
@@ -308,26 +314,24 @@
         work=23000000000,
     )
     far_pack = shaped(N_FAR_PACK, 64, 128)
-    to_even, to_odd, other = call(
+    received = swapped(other)
+    to_even, to_odd = call(
         "pack",
         pack_kernel,
-        "vvva>vva",
-        [far_pack, far_pack, shaped(32, 64, 256)],
+        "vvv>vv",
+        [far_pack, far_pack],
         even,
         pack,
         odd,
-        other,
-        alias={3: 2},
-    )
-    received = swapped(other)
+        work=11500000000,
+    )
     far_even, far_odd = paired(to_even, 3, 0), paired(to_odd, 3, 1)
     halos = shaped(8, 64, 256)
     [far] = call(
         "leaf",
         leaf_kernel,
-        "sssvvvv>v",
+        "ssvvvv>v",
         [shaped(16, 64, 64, dtype=F32)],
-        near_row,
         list_leaf,
         count_leaf,
         pack,
@@ -340,9 +344,8 @@
     halo_even, halo_odd = call(
         "halo",
         halo_kernel,
-        "svv>vv",
+        "vv>vv",
         [halos] * 2,
-        near_row,
         acc,
         received,
     )
@@ -350,9 +353,8 @@
     [down_middle] = call(
         "tops",
         tops_kernel,
-        "sssssvvvvvvvva>v",
+        "ssssvvvvvvvva>v",
         [shaped(8, 64, 64)],
-        near_row,
         list_middle,
         list_top,
         count_middle,
@@ -385,9 +387,8 @@
     [out] = call(
         "final",
         final_kernel,
-        "svvv>v",
+        "vvv>v",
         [shaped(64, 4096)],
-        near_row,
         total,
         from_even,
         from_odd,

time: 41 us -> 33.7 us (0.82); the launches traced: 40.9 us -> 33.1 us
  starting transfers between devices: 18 us -> 12.6 us
  Pallas kernels: 15.1 us -> 13.9 us
  waiting for transfers between devices: 7.31 us -> 6.37 us
    ppermute x6, starting transfers between devices: 18 us -> 12.3 us  [paired(): return lax.ppermute(block, ('leaf', 'rhs'), route)]
    pallas_call x8, Pallas kernels: 15.1 us -> 13.9 us  [call(): pl.pallas_call(kernel, name=name, in_specs=[specs[k] for k in kinds], out...]
    ppermute x6, waiting for transfers between devices: 7.3 us -> 6.37 us  [paired(): return lax.ppermute(block, ('leaf', 'rhs'), route)]
  transfers between devices with their start and end apart: 8 -> 8, of which waited for: 2 -> 4; matrix products, arithmetic and copies ran while one was open for 0% -> 0% of each run, Pallas kernels for 33% -> 39%
where the time goes in v3:
time: 33.7 us; the launch traced here: 33.1 us
  Pallas kernels  13.9 us (41%)
  starting transfers between devices  12.6 us (37%)
  waiting for transfers between devices  6.37 us (19%)
    pallas_call x8, Pallas kernels, call(): pl.pallas_call(kernel, name=name, in_specs=[specs[k] for k in kinds], out...  13.9 us
    ppermute x6, starting transfers between devices, paired(): return lax.ppermute(block, ('leaf', 'rhs'), route)  12.3 us
    ppermute x6, waiting for transfers between devices, paired(): return lax.ppermute(block, ('leaf', 'rhs'), route)  6.37 us
  transfers between devices with their start and end apart: 8, of which 4 were waited for; matrix products, arithmetic and copies ran while one was open for 0% of the time, Pallas kernels for 39%

profile of v3, /device:TPU:16, one launch (start us, length us, event | category | flops | bytes accessed | tf_op | source)
XLA Modules:
  0.0 33.1 jit_solution(892031626542370905)
XLA Ops:
  0.0 0.0 collective-permute-start.4
  0.0 3.4 %coeff.1 = (bf16[14,64,128]{2,1,0:T(8,128)(2,1)S(1)}, bf16[64,4096]{1,0:T(8,128)(2,1)S(1)}, bf16[16,256,256]{2,1,0:T(8,128)(2,1)S(1)}) custom-call(bf16[64,4096]{1,0:T(8,128)(2,1)} %bitcast.15, bf16[16,64,256]{2,1,0:T(8,128)(2,1)} %bitcast.13, bf16[8,128,64]{2,1,0:T(8,128)(2,1)} %bitcast.16, bf16[4,128,64]{2,1,0:T(8,128)(2,1)} %bitcast.17, ...), custom_call_target="tpu_custom_call" | custom-call | tf_op jit(solution)/shard_map/coeff/pallas_call | solution.py:241
  3.4 6.2 %collective-permute-start.1 = (bf16[14,64,128]{2,1,0:T(8,128)(2,1)S(1)}, bf16[14,64,128]{2,1,0:T(8,128)(2,1)S(1)}, u32[]{:S(2)}, u32[]{:S(2)}) collective-permute-start(bf16[14,64,128]{2,1,0:T(8,128)(2,1)S(1)} %get-tuple-element.14.pack.own), channel_id=1, source_target_pairs={{0,1},{1,0},{2,4},{3,5},{4,2},{5,3},{6,8},{7,9},{8,6},{9,7},{10,12... | collective-permute-start | bytes 688136 | tf_op jit(solution)/shard_map/ppermute | solution.py:42
  9.6 3.7 %near.1 = (f32[32,128,256]{2,1,0:T(8,128)S(1)}, bf16[32,64,256]{2,1,0:T(8,128)(2,1)S(1)}) custom-call(s32[64]{0:T(128)} %row_at.1, s32[64]{0:T(128)} %col_at.1, bf16[64,4096]{1,0:T(8,128)(2,1)S(1)} %get-tuple-element.17.x, bf16[64,4096]{1,0:T(8,128)(2,1)S(1)} %collective-permute-done.4.xp, bf16[16,256,256]{2,1,0:T(8,128)(2,1)S(1)} %get-tuple-element.18.held, ...), custom_call_target="tpu_custom_call" | custom-call | flops 23000000512 | bytes 76666664 | tf_op jit(solution)/shard_map/near/pallas_call | solution.py:241
  13.4 0.3 collective-permute-start.5
  13.7 2.2 %collective-permute-done.1.odd = bf16[14,64,128]{2,1,0:T(8,128)(2,1)S(1)} collective-permute-done((bf16[14,64,128]{2,1,0:T(8,128)(2,1)S(1)}, bf16[14,64,128]{2,1,0:T(8,128)(2,1)S(1)}, u32[]{:S(2)}, u32[]{:S(2)}) %collective-permute-start.1) | collective-permute-done | bytes 229408 | tf_op jit(solution)/shard_map/ppermute | solution.py:42
  15.9 1.5 %collective-permute-done.even = bf16[14,64,128]{2,1,0:T(8,128)(2,1)S(1)} collective-permute-done((bf16[14,64,128]{2,1,0:T(8,128)(2,1)S(1)}, bf16[14,64,128]{2,1,0:T(8,128)(2,1)S(1)}, u32[]{:S(2)}, u32[]{:S(2)}) %collective-permute-start) | collective-permute-done | bytes 229408 | tf_op jit(solution)/shard_map/ppermute | solution.py:42
  17.4 0.0 copy-start.9
  17.4 0.0 copy-start.10
  17.4 0.0 copy-start.11
  17.4 0.4 %collective-permute-start.2 = (bf16[10,64,128]{2,1,0:T(8,128)(2,1)S(1)}, bf16[10,64,128]{2,1,0:T(8,128)(2,1)S(1)}, u32[]{:S(2)}, u32[]{:S(2)}) collective-permute-start(bf16[10,64,128]{2,1,0:T(8,128)(2,1)S(1)} %get-tuple-element.15), channel_id=1, source_target_pairs={{0,6},{1,7},{2,3},{3,2},{4,10},{5,11},{6,0},{7,1},{8,14},{9,15},{1... | collective-permute-start | bytes 491528 | tf_op jit(solution)/shard_map/ppermute | solution.py:42
  17.8 0.3 collective-permute-start.3
  18.1 0.0 collective-permute-done.5.received
  18.1 0.1 halo.1
  18.2 2.7 %collective-permute-start.6 = (bf16[8,64,256]{2,1,0:T(8,128)(2,1)S(1)}, bf16[8,64,256]{2,1,0:T(8,128)(2,1)S(1)}, u32[]{:S(2)}, u32[]{:S(2)}) collective-permute-start(bf16[8,64,256]{2,1,0:T(8,128)(2,1)S(1)} %get-tuple-element.21), channel_id=1, source_target_pairs={{0,2},{1,3},{2,0},{3,1},{4,6},{5,7},{6,4},{7,5},{8,10},{9,11},{10,... | collective-permute-start | bytes 786440 | tf_op jit(solution)/shard_map/ppermute | solution.py:42
  20.9 2.7 %collective-permute-start.7 = (bf16[8,64,256]{2,1,0:T(8,128)(2,1)S(1)}, bf16[8,64,256]{2,1,0:T(8,128)(2,1)S(1)}, u32[]{:S(2)}, u32[]{:S(2)}) collective-permute-start(bf16[8,64,256]{2,1,0:T(8,128)(2,1)S(1)} %get-tuple-element.22), channel_id=1, source_target_pairs={{0,1},{1,0},{2,4},{3,5},{4,2},{5,3},{6,8},{7,9},{8,6},{9,7},{10,12... | collective-permute-start | bytes 786440 | tf_op jit(solution)/shard_map/ppermute | solution.py:42
  23.6 0.0 copy-start.1
  23.6 0.0 copy-start.4
  23.6 0.0 copy-start.5
  23.6 0.0 copy-start.6
  23.7 0.0 copy-start.7
  23.7 0.0 copy-start.8
  23.7 1.7 %leaf.1.after.far = f32[16,64,64]{2,1,0:T(8,128)S(1)} custom-call(s32[16,16]{1,0:T(8,128)S(1)} %copy-done.10, s32[16]{0:T(128)S(1)} %copy-done.11, bf16[14,64,128]{2,1,0:T(8,128)(2,1)S(1)} %get-tuple-element.14.pack.own, bf16[14,64,128]{2,1,0:T(8,128)(2,1)S(1)} %collective-permute-done.even, bf16[14,64,128]{2,1,0:T(8,128)(2,1)S(1)} %collective-permute-done.1.odd, ...), custom_call_target="tpu_custom_call" | custom-call | flops 23000000512 | bytes 76666664 | tf_op jit(solution)/shard_map/leaf/pallas_call | solution.py:241
  25.4 0.0 copy-start.2
  25.4 0.0 copy-start.3
  25.5 0.0 collective-permute-done.2.far_even
  25.5 1.0 %collective-permute-done.3.far_odd = bf16[10,64,128]{2,1,0:T(8,128)(2,1)S(1)} collective-permute-done((bf16[10,64,128]{2,1,0:T(8,128)(2,1)S(1)}, bf16[10,64,128]{2,1,0:T(8,128)(2,1)S(1)}, u32[]{:S(2)}, u32[]{:S(2)}) %collective-permute-start.3) | collective-permute-done | bytes 163872 | tf_op jit(solution)/shard_map/ppermute | solution.py:42
  26.5 1.7 %tops.1.down_middle = bf16[8,64,64]{2,1,0:T(8,128)(2,1)S(1)} custom-call(s32[8,16]{1,0:T(8,128)S(1)} %copy-done.5, s32[4,16]{1,0:T(4,128)S(1)} %copy-done.6, s32[8]{0:T(128)S(1)} %copy-done.7, s32[4]{0:T(128)S(1)} %copy-done.8, bf16[14,64,128]{2,1,0:T(8,128)(2,1)S(1)} %get-tuple-element.14.pack.own, bf16[14,64,128]{2,1,0:T(8,128)(2,1)S(1)} %collective-permute-done.even, ...), custom_call_target="tpu_custom_call" | custom-call | flops 1150000000 | bytes 3833333 | tf_op jit(solution)/shard_map/tops/pallas_call | solution.py:241
  28.2 2.3 %finish.1.total = f32[16,64,256]{2,1,0:T(8,128)S(1)} custom-call(f32[16,64,64]{2,1,0:T(8,128)S(1)} %leaf.1.after.far, bf16[8,64,64]{2,1,0:T(8,128)(2,1)S(1)} %tops.1.down_middle, bf16[16,64,64]{2,1,0:T(8,128)(2,1)S(1)} %copy-done.3, bf16[16,64,256]{2,1,0:T(8,128)(2,1)S(1)} %bitcast.11, f32[32,128,256]{2,1,0:T(8,128)S(1)} %get-tuple-element.19.acc, ...), custom_call_target="tpu_custom_call" | custom-call | flops 1150000000 | bytes 3833333 | tf_op jit(solution)/shard_map/finish/pallas_call | solution.py:241
  30.5 0.0 collective-permute-done.6.from_even
  30.5 1.7 %collective-permute-done.7.from_odd = bf16[8,64,256]{2,1,0:T(8,128)(2,1)S(1)} collective-permute-done((bf16[8,64,256]{2,1,0:T(8,128)(2,1)S(1)}, bf16[8,64,256]{2,1,0:T(8,128)(2,1)S(1)}, u32[]{:S(2)}, u32[]{:S(2)}) %collective-permute-start.7) | collective-permute-done | bytes 262176 | tf_op jit(solution)/shard_map/ppermute | solution.py:42
  32.3 0.9 %final.1 = bf16[64,4096]{1,0:T(8,128)(2,1)} custom-call(f32[16,64,256]{2,1,0:T(8,128)S(1)} %finish.1.total, bf16[8,64,256]{2,1,0:T(8,128)(2,1)S(1)} %collective-permute-done.6.from_even, bf16[8,64,256]{2,1,0:T(8,128)(2,1)S(1)} %collective-permute-done.7.from_odd), custom_call_target="tpu_custom_call" | custom-call | tf_op jit(solution)/shard_map/final/pallas_call | solution.py:241
  (16 shorter events, 0.1 us)
Async XLA Ops:
  0.0 9.6 %collective-permute-start.4 = (bf16[64,4096]{1,0:T(8,128)(2,1)}, bf16[64,4096]{1,0:T(8,128)(2,1)S(1)}, u32[]{:S(2)}, u32[]{:S(2)}) collective-permute-start(bf16[64,4096]{1,0:T(8,128)(2,1)} %bitcast.14), channel_id=1, source_target_pairs={{0,1},{1,0},{2,3},{3,2},{4,5},{5,4},{6,7},{7,6},{8,9},{9,8},{10,11... | collective-permute-start | bytes 1572872 | tf_op jit(solution)/shard_map/ppermute | solution.py:46
  3.4 12.5 %collective-permute-start.1 = (bf16[14,64,128]{2,1,0:T(8,128)(2,1)S(1)}, bf16[14,64,128]{2,1,0:T(8,128)(2,1)S(1)}, u32[]{:S(2)}, u32[]{:S(2)}) collective-permute-start(bf16[14,64,128]{2,1,0:T(8,128)(2,1)S(1)} %get-tuple-element.14.pack.own), channel_id=1, source_target_pairs={{0,1},{1,0},{2,4},{3,5},{4,2},{5,3},{6,8},{7,9},{8,6},{9,7},{10,12... | collective-permute-start | bytes 688136 | tf_op jit(solution)/shard_map/ppermute | solution.py:42
  9.6 7.7 %collective-permute-start = (bf16[14,64,128]{2,1,0:T(8,128)(2,1)S(1)}, bf16[14,64,128]{2,1,0:T(8,128)(2,1)S(1)}, u32[]{:S(2)}, u32[]{:S(2)}) collective-permute-start(bf16[14,64,128]{2,1,0:T(8,128)(2,1)S(1)} %get-tuple-element.14.pack.own), channel_id=1, source_target_pairs={{0,2},{1,3},{2,0},{3,1},{4,6},{5,7},{6,4},{7,5},{8,10},{9,11},{10,... | collective-permute-start | bytes 688136 | tf_op jit(solution)/shard_map/ppermute | solution.py:42
  13.4 4.8 %collective-permute-start.5 = (bf16[32,64,256]{2,1,0:T(8,128)(2,1)S(1)}, bf16[32,64,256]{2,1,0:T(8,128)(2,1)S(1)}, u32[]{:S(2)}, u32[]{:S(2)}) collective-permute-start(bf16[32,64,256]{2,1,0:T(8,128)(2,1)S(1)} %get-tuple-element.20), channel_id=1, source_target_pairs={{0,1},{1,0},{2,3},{3,2},{4,5},{5,4},{6,7},{7,6},{8,9},{9,8},{10,11... | collective-permute-start | bytes 3145736 | tf_op jit(solution)/shard_map/ppermute | solution.py:46
  17.4 6.2 %copy-start.9 = (bf16[16,16,64,64]{3,2,1,0:T(8,128)(2,1)S(1)}, bf16[16,16,64,64]{3,2,1,0:T(8,128)(2,1)}, u32[]{:S(2)}) copy-start(bf16[16,16,64,64]{3,2,1,0:T(8,128)(2,1)} %param.29) | copy-start | bytes 6291460
  17.4 6.2 %copy-start.10 = (s32[16,16]{1,0:T(8,128)S(1)}, s32[16,16]{1,0:T(8,128)}, u32[]{:S(2)}) copy-start(s32[16,16]{1,0:T(8,128)} %lists.1) | copy-start | bytes 3076
  17.4 6.2 %copy-start.11 = (s32[16]{0:T(128)S(1)}, s32[16]{0:T(128)}, u32[]{:S(2)}) copy-start(s32[16]{0:T(128)} %counts.1) | copy-start | bytes 196
  17.4 8.1 %collective-permute-start.2 = (bf16[10,64,128]{2,1,0:T(8,128)(2,1)S(1)}, bf16[10,64,128]{2,1,0:T(8,128)(2,1)S(1)}, u32[]{:S(2)}, u32[]{:S(2)}) collective-permute-start(bf16[10,64,128]{2,1,0:T(8,128)(2,1)S(1)} %get-tuple-element.15), channel_id=1, source_target_pairs={{0,6},{1,7},{2,3},{3,2},{4,10},{5,11},{6,0},{7,1},{8,14},{9,15},{1... | collective-permute-start | bytes 491528 | tf_op jit(solution)/shard_map/ppermute | solution.py:42
  17.8 8.7 %collective-permute-start.3 = (bf16[10,64,128]{2,1,0:T(8,128)(2,1)S(1)}, bf16[10,64,128]{2,1,0:T(8,128)(2,1)S(1)}, u32[]{:S(2)}, u32[]{:S(2)}) collective-permute-start(bf16[10,64,128]{2,1,0:T(8,128)(2,1)S(1)} %get-tuple-element.16), channel_id=1, source_target_pairs={{0,5},{1,4},{2,8},{3,9},{4,1},{5,0},{6,12},{7,13},{8,2},{9,3},{10,... | collective-permute-start | bytes 491528 | tf_op jit(solution)/shard_map/ppermute | solution.py:42
  18.2 12.3 %collective-permute-start.6 = (bf16[8,64,256]{2,1,0:T(8,128)(2,1)S(1)}, bf16[8,64,256]{2,1,0:T(8,128)(2,1)S(1)}, u32[]{:S(2)}, u32[]{:S(2)}) collective-permute-start(bf16[8,64,256]{2,1,0:T(8,128)(2,1)S(1)} %get-tuple-element.21), channel_id=1, source_target_pairs={{0,2},{1,3},{2,0},{3,1},{4,6},{5,7},{6,4},{7,5},{8,10},{9,11},{10,... | collective-permute-start | bytes 786440 | tf_op jit(solution)/shard_map/ppermute | solution.py:42
  20.9 11.3 %collective-permute-start.7 = (bf16[8,64,256]{2,1,0:T(8,128)(2,1)S(1)}, bf16[8,64,256]{2,1,0:T(8,128)(2,1)S(1)}, u32[]{:S(2)}, u32[]{:S(2)}) collective-permute-start(bf16[8,64,256]{2,1,0:T(8,128)(2,1)S(1)} %get-tuple-element.22), channel_id=1, source_target_pairs={{0,1},{1,0},{2,4},{3,5},{4,2},{5,3},{6,8},{7,9},{8,6},{9,7},{10,12... | collective-permute-start | bytes 786440 | tf_op jit(solution)/shard_map/ppermute | solution.py:42
  23.6 2.9 %copy-start = (bf16[8,16,64,64]{3,2,1,0:T(8,128)(2,1)S(1)}, bf16[8,16,64,64]{3,2,1,0:T(8,128)(2,1)}, u32[]{:S(2)}) copy-start(bf16[8,16,64,64]{3,2,1,0:T(8,128)(2,1)} %param.30) | copy-start | bytes 3145732
  23.6 2.9 %copy-start.1 = (bf16[4,16,64,64]{3,2,1,0:T(8,128)(2,1)S(1)}, bf16[4,16,64,64]{3,2,1,0:T(8,128)(2,1)}, u32[]{:S(2)}) copy-start(bf16[4,16,64,64]{3,2,1,0:T(8,128)(2,1)} %param.31) | copy-start | bytes 1572868
  23.6 2.9 %copy-start.4 = (bf16[8,64,64]{2,1,0:T(8,128)(2,1)S(1)}, bf16[8,64,64]{2,1,0:T(8,128)(2,1)}, u32[]{:S(2)}) copy-start(bf16[8,64,64]{2,1,0:T(8,128)(2,1)} %spread_middle.1) | copy-start | bytes 196612
  23.6 2.9 %copy-start.5 = (s32[8,16]{1,0:T(8,128)S(1)}, s32[8,16]{1,0:T(8,128)}, u32[]{:S(2)}) copy-start(s32[8,16]{1,0:T(8,128)} %list_middle.1) | copy-start | bytes 1540
  23.6 2.8 %copy-start.6 = (s32[4,16]{1,0:T(4,128)S(1)}, s32[4,16]{1,0:T(4,128)}, u32[]{:S(2)}) copy-start(s32[4,16]{1,0:T(4,128)} %list_top.1) | copy-start | bytes 772
  23.7 2.8 %copy-start.7 = (s32[8]{0:T(128)S(1)}, s32[8]{0:T(128)}, u32[]{:S(2)}) copy-start(s32[8]{0:T(128)} %count_middle.1) | copy-start | bytes 100
  23.7 2.8 %copy-start.8 = (s32[4]{0:T(128)S(1)}, s32[4]{0:T(128)}, u32[]{:S(2)}) copy-start(s32[4]{0:T(128)} %count_top.1) | copy-start | bytes 52
  25.4 2.8 %copy-start.2 = (bf16[16,256,64]{1,2,0:T(8,128)(2,1)S(1)}, bf16[16,256,64]{1,2,0:T(8,128)(2,1)}, u32[]{:S(2)}) copy-start(bf16[16,256,64]{1,2,0:T(8,128)(2,1)} %param.24) | copy-start | bytes 1572868
  25.4 2.8 %copy-start.3 = (bf16[16,64,64]{2,1,0:T(8,128)(2,1)S(1)}, bf16[16,64,64]{2,1,0:T(8,128)(2,1)}, u32[]{:S(2)}) copy-start(bf16[16,64,64]{2,1,0:T(8,128)(2,1)} %spread_leaf.1) | copy-start | bytes 393220

commit v4 on v3

--- a/solution.py
+++ b/solution.py
@@ -15,7 +15,6 @@
 N_PACK = 14
 N_FAR_PACK = 10
 CHUNKS = 8
-FIRST = 16
 TOP_AT = 40
 ZERO_AT = TOP_AT + 36
 
@@ -65,40 +64,50 @@
     return made
 
 
+def mm_first(a, b):
+    return lax.dot_general(a, b, (((0,), (0,)), ((), ())), preferred_element_type=F32)
+
+
 def coeff_kernel(
-    x_at, basis_at, lift_leaf_at, lift_middle_at, blocks, pack, x, held, basis, lift_leaf, lift_middle, sems
+    x_at, basis_at, lift_leaf_at, lift_middle_at, pack, x, basis, lift_leaf, lift_middle, sems
 ):
-    copies = started(
-        (x_at, x, sems.at[0]),
-        (basis_at, basis, sems.at[1]),
-        (lift_leaf_at, lift_leaf, sems.at[2]),
-        (lift_middle_at, lift_middle, sems.at[3]),
-        (blocks.at[pl.ds(0, FIRST)], held, sems.at[4]),
-    )
-    for c in copies[:4]:
-        c.wait()
+    parts = []
     for q in range(4):
-        middles = []
+        columns, leaves = pl.ds(q * 1024, 1024), pl.ds(q * 4, 4)
+        parts.append(
+            started(
+                (x_at.at[:, columns], x.at[:, columns], sems.at[2 * q]),
+                (basis_at.at[leaves], basis.at[leaves], sems.at[2 * q + 1]),
+            )
+        )
+        if q == 0:
+            lifts = started(
+                (lift_leaf_at, lift_leaf, sems.at[8]), (lift_middle_at, lift_middle, sems.at[9])
+            )
+    for q in range(4):
+        for c in parts[q]:
+            c.wait()
         for p in (2 * q, 2 * q + 1):
             pair = [
                 mm_t(x[:, l * 256 : (l + 1) * 256], basis[l]) for l in (2 * p, 2 * p + 1)
             ]
-            block = jnp.concatenate(pair, axis=1).astype(BF16)
-            pack[p] = block
-            middles.append(mm(block, lift_leaf[p]))
+            pack[p] = jnp.concatenate(pair, axis=1).astype(BF16)
+    for c in lifts:
+        c.wait()
+    for q in range(4):
+        middles = [mm(pack[p], lift_leaf[p]) for p in (2 * q, 2 * q + 1)]
         pack[8 + q] = jnp.concatenate(middles, axis=1).astype(BF16)
     for h in range(2):
         tops = [mm(pack[8 + q], lift_middle[q]) for q in (2 * h, 2 * h + 1)]
         pack[12 + h] = jnp.concatenate(tops, axis=1).astype(BF16)
-    copies[4].wait()
-
-
-def near_kernel(row_at, col_at, x, xp, held, blocks, acc, other, row, col, rest, sems):
-    per = rest.shape[0] // CHUNKS
+
+
+def near_kernel(row_at, col_at, x, xp, blocks, acc, other, row, col, held, sems):
+    per = held.shape[0] // CHUNKS
     places = started((row_at, row, sems.at[CHUNKS]), (col_at, col, sems.at[CHUNKS + 1]))
     copies = started(
         *[
-            (blocks.at[pl.ds(FIRST + c * per, per)], rest.at[pl.ds(c * per, per)], sems.at[c])
+            (blocks.at[pl.ds(c * per, per)], held.at[pl.ds(c * per, per)], sems.at[c])
             for c in range(CHUNKS)
         ]
     )
@@ -106,13 +115,13 @@
     for c in places:
         c.wait()
     device, _ = place()
-    for b in range(blocks.shape[0]):
-        if b >= FIRST and (b - FIRST) % per == 0:
-            copies[(b - FIRST) // per].wait()
+    for b in range(held.shape[0]):
+        if b % per == 0:
+            copies[b // per].wait()
         at = pl.multiple_of((row[b] - device * 16) * 256, 256)
         slot = col[b] - device * 16 + 8
         left = jnp.concatenate([x[:, pl.ds(at, 256)], xp[:, pl.ds(at, 256)]], axis=0)
-        acc[slot] += mm(left, held[b] if b < FIRST else rest[b - FIRST])
+        acc[slot] += mm(left, held[b])
     other[...] = acc[:, 64:].astype(BF16)
 
 
@@ -153,14 +162,18 @@
     return mm(gathered, couple[t])
 
 
-def leaf_kernel(lists, counts, pack, even, odd, couple, far, dup):
+def leaf_kernel(
+    lists, counts, pack, even, odd, couple, spread, bases, acc, received, begun, joined, dup
+):
     device, side = place()
     for i in range(8):
         for step, ref in ((0, pack), (side, even), (-side, odd)):
             double(dup, 16 * (1 + step) + 2 * i, ref[i])
     dup[48] = jnp.zeros((64, 128), BF16)
     for t in range(16):
-        far[t] = coupled(dup, 48, couple, lists, counts, t, 16 - 16 * device)
+        far = coupled(dup, 48, couple, lists, counts, t, 16 - 16 * device).astype(BF16)
+        begun[t] = mm(far, bases[t]) + (acc[8 + t, :64] + received[8 + t].astype(F32))
+        joined[t] = mm_first(spread[t], bases[t]).astype(BF16)
 
 
 def halo_kernel(acc, received, to_even, to_odd):
@@ -183,8 +196,9 @@
     couple_middle,
     couple_top,
     spread_middle,
-    after,
-    down_middle,
+    begun,
+    joined,
+    total,
     dup,
 ):
     device, side = place()
@@ -210,16 +224,12 @@
         for t in range(4)
     ]
     for t in range(8):
-        down_middle[t] = (
+        down_middle = (
             coupled(dup, ZERO_AT, couple_middle, list_middle, count_middle, t, 16 - 8 * device)
             + mm_t(down_top[t // 2], spread_middle[t])
         ).astype(BF16)
-
-
-def finish_kernel(far, down_middle, spread_leaf, bases, acc, received, out):
-    for t in range(16):
-        down = (far[t] + mm_t(down_middle[t // 2], spread_leaf[t])).astype(BF16)
-        out[t] = mm(down, bases[t]) + (acc[8 + t, :64] + received[8 + t].astype(F32))
+        for l in (2 * t, 2 * t + 1):
+            total[l] = begun[l] + mm(down_middle, joined[l])
 
 
 def final_kernel(total, from_even, from_odd, out):
@@ -274,40 +284,37 @@
 ):
     x = operand.T
     xp = swapped(x)
-    blocks = in_hbm(near_blocks)
-    pack, x_held, held = call(
+    pack, x_held = call(
         "coeff",
         coeff_kernel,
-        "hhhhh>vvv",
-        [shaped(N_PACK, 64, 128), shaped(64, 4096), shaped(FIRST, 256, 256)],
+        "hhhh>vv",
+        [shaped(N_PACK, 64, 128), shaped(64, 4096)],
         in_hbm(x),
         in_hbm(jnp.swapaxes(row_basis, 1, 2)),
         in_hbm(lift_leaf.reshape(8, 128, 64)),
         in_hbm(lift_middle.reshape(4, 128, 64)),
-        blocks,
         scratch=[
             pltpu.VMEM((16, 64, 256), BF16),
             pltpu.VMEM((8, 128, 64), BF16),
             pltpu.VMEM((4, 128, 64), BF16),
-            pltpu.SemaphoreType.DMA((5,)),
+            pltpu.SemaphoreType.DMA((10,)),
         ],
     )
     even, odd = paired(pack, 1, 0), paired(pack, 1, 1)
     acc, other = call(
         "near",
         near_kernel,
-        "hhvvvh>vv",
+        "hhvvh>vv",
         [shaped(32, 128, 256, dtype=F32), shaped(32, 64, 256)],
         in_hbm(near_row),
         in_hbm(near_column),
         x_held,
         xp,
-        held,
-        blocks,
+        in_hbm(near_blocks),
         scratch=[
             pltpu.SMEM((64,), jnp.int32),
             pltpu.SMEM((64,), jnp.int32),
-            pltpu.VMEM((64 - FIRST, 256, 256), BF16),
+            pltpu.VMEM((64, 256, 256), BF16),
             pltpu.SemaphoreType.DMA((CHUNKS + 2,)),
         ],
         mib=16,
@@ -327,17 +334,22 @@
     )
     far_even, far_odd = paired(to_even, 3, 0), paired(to_odd, 3, 1)
     halos = shaped(8, 64, 256)
-    [far] = call(
+    sums = shaped(16, 64, 256, dtype=F32)
+    begun, joined = call(
         "leaf",
         leaf_kernel,
-        "ssvvvv>v",
-        [shaped(16, 64, 64, dtype=F32)],
+        "ssvvvvvvvv>vv",
+        [sums, shaped(16, 64, 256)],
         list_leaf,
         count_leaf,
         pack,
         even,
         odd,
         couple_leaf.reshape(16, 1024, 64),
+        spread_leaf,
+        jnp.swapaxes(leaf_column_bases, 1, 2),
+        acc,
+        received,
         scratch=[pltpu.VMEM((49, 64, 128), BF16)],
         work=23000000000,
     )
@@ -350,11 +362,11 @@
         received,
     )
     from_even, from_odd = paired(halo_even, 1, 0), paired(halo_odd, 1, 1)
-    [down_middle] = call(
+    [total] = call(
         "tops",
         tops_kernel,
-        "ssssvvvvvvvva>v",
-        [shaped(8, 64, 64)],
+        "ssssvvvvvvvvvv>v",
+        [sums],
         list_middle,
         list_top,
         count_middle,
@@ -367,22 +379,10 @@
         couple_middle.reshape(8, 1024, 64),
         couple_top.reshape(4, 1024, 64),
         spread_middle,
-        far,
+        begun,
+        joined,
         scratch=[pltpu.VMEM((ZERO_AT + 1, 64, 128), BF16)],
-        work=1150000000,
-    )
-    [total] = call(
-        "finish",
-        finish_kernel,
-        "vvvvvv>v",
-        [shaped(16, 64, 256, dtype=F32)],
-        far,
-        down_middle,
-        spread_leaf,
-        jnp.swapaxes(leaf_column_bases, 1, 2),
-        acc,
-        received,
-        work=1150000000,
+        work=2300000000,
     )
     [out] = call(
         "final",

time: 33.7 us -> 32.6 us (0.967)
  waiting for transfers between devices: 6.37 us -> 5.54 us
    ppermute x6, waiting for transfers between devices: 6.37 us -> 5.54 us  [paired(): return lax.ppermute(block, ('leaf', 'rhs'), route)]
    pallas_call x8 -> x7, Pallas kernels: 13.9 us -> 13.9 us  [call(): pl.pallas_call(kernel, name=name, in_specs=[specs[k] for k in kinds], out...]
  transfers between devices with their start and end apart: 8 -> 8, of which waited for: 4 -> 3; matrix products, arithmetic and copies ran while one was open for 0% -> 0% of each run, Pallas kernels for 39% -> 40%
where the time goes in v4:
time: 32.6 us; the launch traced here: 32.3 us
  Pallas kernels  13.9 us (43%)
  starting transfers between devices  12.6 us (39%)
  waiting for transfers between devices  5.54 us (17%)
    pallas_call x7, Pallas kernels, call(): pl.pallas_call(kernel, name=name, in_specs=[specs[k] for k in kinds], out...  13.9 us
    ppermute x6, starting transfers between devices, paired(): return lax.ppermute(block, ('leaf', 'rhs'), route)  12.3 us
    ppermute x6, waiting for transfers between devices, paired(): return lax.ppermute(block, ('leaf', 'rhs'), route)  5.54 us
  transfers between devices with their start and end apart: 8, of which 3 were waited for; matrix products, arithmetic and copies ran while one was open for 0% of the time, Pallas kernels for 40%

profile of v4, /device:TPU:16, one launch (start us, length us, event | category | flops | bytes accessed | tf_op | source)
XLA Modules:
  0.0 32.3 jit_solution(17040035580538630861)
XLA Ops:
  0.0 2.5 %coeff.1 = (bf16[14,64,128]{2,1,0:T(8,128)(2,1)S(1)}, bf16[64,4096]{1,0:T(8,128)(2,1)S(1)}) custom-call(bf16[64,4096]{1,0:T(8,128)(2,1)} %bitcast.15, bf16[16,64,256]{2,1,0:T(8,128)(2,1)} %bitcast.13, bf16[8,128,64]{2,1,0:T(8,128)(2,1)} %bitcast.16, bf16[4,128,64]{2,1,0:T(8,128)(2,1)} %bitcast.17), custom_call_target="tpu_custom_call" | custom-call | tf_op jit(solution)/shard_map/coeff/pallas_call | solution.py:251
  2.5 6.2 %collective-permute-start.1 = (bf16[14,64,128]{2,1,0:T(8,128)(2,1)S(1)}, bf16[14,64,128]{2,1,0:T(8,128)(2,1)S(1)}, u32[]{:S(2)}, u32[]{:S(2)}) collective-permute-start(bf16[14,64,128]{2,1,0:T(8,128)(2,1)S(1)} %get-tuple-element.15.own.pack), channel_id=1, source_target_pairs={{0,1},{1,0},{2,4},{3,5},{4,2},{5,3},{6,8},{7,9},{8,6},{9,7},{10,12... | collective-permute-start | bytes 688136 | tf_op jit(solution)/shard_map/ppermute | solution.py:41
  8.7 0.0 collective-permute-start
  8.7 0.0 collective-permute-done.4.xp
  8.7 4.1 %near.1 = (f32[32,128,256]{2,1,0:T(8,128)S(1)}, bf16[32,64,256]{2,1,0:T(8,128)(2,1)S(1)}) custom-call(s32[64]{0:T(128)} %row_at.1, s32[64]{0:T(128)} %col_at.1, bf16[64,4096]{1,0:T(8,128)(2,1)S(1)} %get-tuple-element.18.x, bf16[64,4096]{1,0:T(8,128)(2,1)S(1)} %collective-permute-done.4.xp, bf16[64,256,256]{2,1,0:T(8,128)(2,1)} %blocks.1), custom_call_target="tpu_custom_call" | custom-call | flops 23000000512 | bytes 76666664 | tf_op jit(solution)/shard_map/near/pallas_call | solution.py:251
  12.8 0.3 %collective-permute-start.5 = (bf16[32,64,256]{2,1,0:T(8,128)(2,1)S(1)}, bf16[32,64,256]{2,1,0:T(8,128)(2,1)S(1)}, u32[]{:S(2)}, u32[]{:S(2)}) collective-permute-start(bf16[32,64,256]{2,1,0:T(8,128)(2,1)S(1)} %get-tuple-element.20), channel_id=1, source_target_pairs={{0,1},{1,0},{2,3},{3,2},{4,5},{5,4},{6,7},{7,6},{8,9},{9,8},{10,11... | collective-permute-start | bytes 3145736 | tf_op jit(solution)/shard_map/ppermute | solution.py:45
  13.1 1.9 %collective-permute-done.1.odd = bf16[14,64,128]{2,1,0:T(8,128)(2,1)S(1)} collective-permute-done((bf16[14,64,128]{2,1,0:T(8,128)(2,1)S(1)}, bf16[14,64,128]{2,1,0:T(8,128)(2,1)S(1)}, u32[]{:S(2)}, u32[]{:S(2)}) %collective-permute-start.1) | collective-permute-done | bytes 229408 | tf_op jit(solution)/shard_map/ppermute | solution.py:41
  15.0 1.5 %collective-permute-done.even = bf16[14,64,128]{2,1,0:T(8,128)(2,1)S(1)} collective-permute-done((bf16[14,64,128]{2,1,0:T(8,128)(2,1)S(1)}, bf16[14,64,128]{2,1,0:T(8,128)(2,1)S(1)}, u32[]{:S(2)}, u32[]{:S(2)}) %collective-permute-start) | collective-permute-done | bytes 229408 | tf_op jit(solution)/shard_map/ppermute | solution.py:41
  16.5 0.0 copy-start
  16.5 0.0 copy-start.3
  16.5 0.0 copy-start.4
  16.5 0.0 copy-start.6
  16.5 0.0 copy-start.9
  16.6 0.4 %collective-permute-start.2 = (bf16[10,64,128]{2,1,0:T(8,128)(2,1)S(1)}, bf16[10,64,128]{2,1,0:T(8,128)(2,1)S(1)}, u32[]{:S(2)}, u32[]{:S(2)}) collective-permute-start(bf16[10,64,128]{2,1,0:T(8,128)(2,1)S(1)} %get-tuple-element.16), channel_id=1, source_target_pairs={{0,6},{1,7},{2,3},{3,2},{4,10},{5,11},{6,0},{7,1},{8,14},{9,15},{1... | collective-permute-start | bytes 491528 | tf_op jit(solution)/shard_map/ppermute | solution.py:41
  16.9 0.3 %collective-permute-start.3 = (bf16[10,64,128]{2,1,0:T(8,128)(2,1)S(1)}, bf16[10,64,128]{2,1,0:T(8,128)(2,1)S(1)}, u32[]{:S(2)}, u32[]{:S(2)}) collective-permute-start(bf16[10,64,128]{2,1,0:T(8,128)(2,1)S(1)} %get-tuple-element.17), channel_id=1, source_target_pairs={{0,5},{1,4},{2,8},{3,9},{4,1},{5,0},{6,12},{7,13},{8,2},{9,3},{10,... | collective-permute-start | bytes 491528 | tf_op jit(solution)/shard_map/ppermute | solution.py:41
  17.3 0.0 collective-permute-done.5.received
  17.3 0.1 halo.1
  17.4 2.7 %collective-permute-start.6 = (bf16[8,64,256]{2,1,0:T(8,128)(2,1)S(1)}, bf16[8,64,256]{2,1,0:T(8,128)(2,1)S(1)}, u32[]{:S(2)}, u32[]{:S(2)}) collective-permute-start(bf16[8,64,256]{2,1,0:T(8,128)(2,1)S(1)} %get-tuple-element.23), channel_id=1, source_target_pairs={{0,2},{1,3},{2,0},{3,1},{4,6},{5,7},{6,4},{7,5},{8,10},{9,11},{10,... | collective-permute-start | bytes 786440 | tf_op jit(solution)/shard_map/ppermute | solution.py:41
  20.1 2.7 %collective-permute-start.7 = (bf16[8,64,256]{2,1,0:T(8,128)(2,1)S(1)}, bf16[8,64,256]{2,1,0:T(8,128)(2,1)S(1)}, u32[]{:S(2)}, u32[]{:S(2)}) collective-permute-start(bf16[8,64,256]{2,1,0:T(8,128)(2,1)S(1)} %get-tuple-element.24), channel_id=1, source_target_pairs={{0,1},{1,0},{2,4},{3,5},{4,2},{5,3},{6,8},{7,9},{8,6},{9,7},{10,12... | collective-permute-start | bytes 786440 | tf_op jit(solution)/shard_map/ppermute | solution.py:41
  22.8 0.0 copy-start.1
  22.8 0.0 copy-start.2
  22.8 0.0 copy-start.5
  22.8 0.0 copy-start.7
  22.8 0.0 copy-start.8
  22.8 0.0 copy-start.10
  22.8 0.0 copy-start.11
  22.9 3.5 %leaf.1 = (f32[16,64,256]{2,1,0:T(8,128)S(1)}, bf16[16,64,256]{2,1,0:T(8,128)(2,1)S(1)}) custom-call(s32[16,16]{1,0:T(8,128)S(1)} %copy-done.6, s32[16]{0:T(128)S(1)} %copy-done.9, bf16[14,64,128]{2,1,0:T(8,128)(2,1)S(1)} %get-tuple-element.15.own.pack, bf16[14,64,128]{2,1,0:T(8,128)(2,1)S(1)} %collective-permute-done.even, ...), custom_call_target="tpu_custom_call" | custom-call | flops 23000000512 | bytes 76666664 | tf_op jit(solution)/shard_map/leaf/pallas_call | solution.py:251
  26.4 0.0 collective-permute-done.2.far_even
  26.5 2.7 %tops.1.total = f32[16,64,256]{2,1,0:T(8,128)S(1)} custom-call(s32[8,16]{1,0:T(8,128)S(1)} %copy-done.7, s32[4,16]{1,0:T(4,128)S(1)} %copy-done.8, s32[8]{0:T(128)S(1)} %copy-done.10, s32[4]{0:T(128)S(1)} %copy-done.11, bf16[14,64,128]{2,1,0:T(8,128)(2,1)S(1)} %get-tuple-element.15.own.pack, bf16[14,64,128]{2,1,0:T(8,128)(2,1)S(1)} %collective-permute-done.even, ...), custom_call_target="tpu_custom_call" | custom-call | flops 2300000000 | bytes 7666666 | tf_op jit(solution)/shard_map/tops/pallas_call | solution.py:251
  29.2 0.0 collective-permute-done.6.from_even
  29.2 2.2 %collective-permute-done.7.from_odd = bf16[8,64,256]{2,1,0:T(8,128)(2,1)S(1)} collective-permute-done((bf16[8,64,256]{2,1,0:T(8,128)(2,1)S(1)}, bf16[8,64,256]{2,1,0:T(8,128)(2,1)S(1)}, u32[]{:S(2)}, u32[]{:S(2)}) %collective-permute-start.7) | collective-permute-done | bytes 262176 | tf_op jit(solution)/shard_map/ppermute | solution.py:41
  31.4 0.9 %final.1 = bf16[64,4096]{1,0:T(8,128)(2,1)} custom-call(f32[16,64,256]{2,1,0:T(8,128)S(1)} %tops.1.total, bf16[8,64,256]{2,1,0:T(8,128)(2,1)S(1)} %collective-permute-done.6.from_even, bf16[8,64,256]{2,1,0:T(8,128)(2,1)S(1)} %collective-permute-done.7.from_odd), custom_call_target="tpu_custom_call" | custom-call | tf_op jit(solution)/shard_map/final/pallas_call | solution.py:251
  (15 shorter events, 0.1 us)
Async XLA Ops:
  0.0 8.7 %collective-permute-start.4 = (bf16[64,4096]{1,0:T(8,128)(2,1)}, bf16[64,4096]{1,0:T(8,128)(2,1)S(1)}, u32[]{:S(2)}, u32[]{:S(2)}) collective-permute-start(bf16[64,4096]{1,0:T(8,128)(2,1)} %bitcast.14), channel_id=1, source_target_pairs={{0,1},{1,0},{2,3},{3,2},{4,5},{5,4},{6,7},{7,6},{8,9},{9,8},{10,11... | collective-permute-start | bytes 1572872 | tf_op jit(solution)/shard_map/ppermute | solution.py:45
  2.5 12.5 %collective-permute-start.1 = (bf16[14,64,128]{2,1,0:T(8,128)(2,1)S(1)}, bf16[14,64,128]{2,1,0:T(8,128)(2,1)S(1)}, u32[]{:S(2)}, u32[]{:S(2)}) collective-permute-start(bf16[14,64,128]{2,1,0:T(8,128)(2,1)S(1)} %get-tuple-element.15.own.pack), channel_id=1, source_target_pairs={{0,1},{1,0},{2,4},{3,5},{4,2},{5,3},{6,8},{7,9},{8,6},{9,7},{10,12... | collective-permute-start | bytes 688136 | tf_op jit(solution)/shard_map/ppermute | solution.py:41
  8.7 7.7 %collective-permute-start = (bf16[14,64,128]{2,1,0:T(8,128)(2,1)S(1)}, bf16[14,64,128]{2,1,0:T(8,128)(2,1)S(1)}, u32[]{:S(2)}, u32[]{:S(2)}) collective-permute-start(bf16[14,64,128]{2,1,0:T(8,128)(2,1)S(1)} %get-tuple-element.15.own.pack), channel_id=1, source_target_pairs={{0,2},{1,3},{2,0},{3,1},{4,6},{5,7},{6,4},{7,5},{8,10},{9,11},{10,... | collective-permute-start | bytes 688136 | tf_op jit(solution)/shard_map/ppermute | solution.py:41
  12.8 4.5 %collective-permute-start.5 = (bf16[32,64,256]{2,1,0:T(8,128)(2,1)S(1)}, bf16[32,64,256]{2,1,0:T(8,128)(2,1)S(1)}, u32[]{:S(2)}, u32[]{:S(2)}) collective-permute-start(bf16[32,64,256]{2,1,0:T(8,128)(2,1)S(1)} %get-tuple-element.20), channel_id=1, source_target_pairs={{0,1},{1,0},{2,3},{3,2},{4,5},{5,4},{6,7},{7,6},{8,9},{9,8},{10,11... | collective-permute-start | bytes 3145736 | tf_op jit(solution)/shard_map/ppermute | solution.py:45
  16.5 6.3 %copy-start = (bf16[16,16,64,64]{3,2,1,0:T(8,128)(2,1)S(1)}, bf16[16,16,64,64]{3,2,1,0:T(8,128)(2,1)}, u32[]{:S(2)}) copy-start(bf16[16,16,64,64]{3,2,1,0:T(8,128)(2,1)} %param.29) | copy-start | bytes 6291460
  16.5 6.3 %copy-start.3 = (bf16[16,256,64]{1,2,0:T(8,128)(2,1)S(1)}, bf16[16,256,64]{1,2,0:T(8,128)(2,1)}, u32[]{:S(2)}) copy-start(bf16[16,256,64]{1,2,0:T(8,128)(2,1)} %param.24) | copy-start | bytes 1572868
  16.5 6.2 %copy-start.4 = (bf16[16,64,64]{2,1,0:T(8,128)(2,1)S(1)}, bf16[16,64,64]{2,1,0:T(8,128)(2,1)}, u32[]{:S(2)}) copy-start(bf16[16,64,64]{2,1,0:T(8,128)(2,1)} %spread.1) | copy-start | bytes 393220
  16.5 6.2 %copy-start.6 = (s32[16,16]{1,0:T(8,128)S(1)}, s32[16,16]{1,0:T(8,128)}, u32[]{:S(2)}) copy-start(s32[16,16]{1,0:T(8,128)} %lists.1) | copy-start | bytes 3076
  16.5 6.2 %copy-start.9 = (s32[16]{0:T(128)S(1)}, s32[16]{0:T(128)}, u32[]{:S(2)}) copy-start(s32[16]{0:T(128)} %counts.1) | copy-start | bytes 196
  16.6 9.8 %collective-permute-start.2 = (bf16[10,64,128]{2,1,0:T(8,128)(2,1)S(1)}, bf16[10,64,128]{2,1,0:T(8,128)(2,1)S(1)}, u32[]{:S(2)}, u32[]{:S(2)}) collective-permute-start(bf16[10,64,128]{2,1,0:T(8,128)(2,1)S(1)} %get-tuple-element.16), channel_id=1, source_target_pairs={{0,6},{1,7},{2,3},{3,2},{4,10},{5,11},{6,0},{7,1},{8,14},{9,15},{1... | collective-permute-start | bytes 491528 | tf_op jit(solution)/shard_map/ppermute | solution.py:41
  16.9 9.4 %collective-permute-start.3 = (bf16[10,64,128]{2,1,0:T(8,128)(2,1)S(1)}, bf16[10,64,128]{2,1,0:T(8,128)(2,1)S(1)}, u32[]{:S(2)}, u32[]{:S(2)}) collective-permute-start(bf16[10,64,128]{2,1,0:T(8,128)(2,1)S(1)} %get-tuple-element.17), channel_id=1, source_target_pairs={{0,5},{1,4},{2,8},{3,9},{4,1},{5,0},{6,12},{7,13},{8,2},{9,3},{10,... | collective-permute-start | bytes 491528 | tf_op jit(solution)/shard_map/ppermute | solution.py:41
  17.4 11.9 %collective-permute-start.6 = (bf16[8,64,256]{2,1,0:T(8,128)(2,1)S(1)}, bf16[8,64,256]{2,1,0:T(8,128)(2,1)S(1)}, u32[]{:S(2)}, u32[]{:S(2)}) collective-permute-start(bf16[8,64,256]{2,1,0:T(8,128)(2,1)S(1)} %get-tuple-element.23), channel_id=1, source_target_pairs={{0,2},{1,3},{2,0},{3,1},{4,6},{5,7},{6,4},{7,5},{8,10},{9,11},{10,... | collective-permute-start | bytes 786440 | tf_op jit(solution)/shard_map/ppermute | solution.py:41
  20.1 11.3 %collective-permute-start.7 = (bf16[8,64,256]{2,1,0:T(8,128)(2,1)S(1)}, bf16[8,64,256]{2,1,0:T(8,128)(2,1)S(1)}, u32[]{:S(2)}, u32[]{:S(2)}) collective-permute-start(bf16[8,64,256]{2,1,0:T(8,128)(2,1)S(1)} %get-tuple-element.24), channel_id=1, source_target_pairs={{0,1},{1,0},{2,4},{3,5},{4,2},{5,3},{6,8},{7,9},{8,6},{9,7},{10,12... | collective-permute-start | bytes 786440 | tf_op jit(solution)/shard_map/ppermute | solution.py:41
  22.8 3.6 %copy-start.1 = (bf16[8,16,64,64]{3,2,1,0:T(8,128)(2,1)S(1)}, bf16[8,16,64,64]{3,2,1,0:T(8,128)(2,1)}, u32[]{:S(2)}) copy-start(bf16[8,16,64,64]{3,2,1,0:T(8,128)(2,1)} %param.30) | copy-start | bytes 3145732
  22.8 3.6 %copy-start.2 = (bf16[4,16,64,64]{3,2,1,0:T(8,128)(2,1)S(1)}, bf16[4,16,64,64]{3,2,1,0:T(8,128)(2,1)}, u32[]{:S(2)}) copy-start(bf16[4,16,64,64]{3,2,1,0:T(8,128)(2,1)} %param.31) | copy-start | bytes 1572868
  22.8 3.6 %copy-start.5 = (bf16[8,64,64]{2,1,0:T(8,128)(2,1)S(1)}, bf16[8,64,64]{2,1,0:T(8,128)(2,1)}, u32[]{:S(2)}) copy-start(bf16[8,64,64]{2,1,0:T(8,128)(2,1)} %spread_middle.1) | copy-start | bytes 196612
  22.8 3.6 %copy-start.7 = (s32[8,16]{1,0:T(8,128)S(1)}, s32[8,16]{1,0:T(8,128)}, u32[]{:S(2)}) copy-start(s32[8,16]{1,0:T(8,128)} %list_middle.1) | copy-start | bytes 1540
  22.8 3.6 %copy-start.8 = (s32[4,16]{1,0:T(4,128)S(1)}, s32[4,16]{1,0:T(4,128)}, u32[]{:S(2)}) copy-start(s32[4,16]{1,0:T(4,128)} %list_top.1) | copy-start | bytes 772
  22.8 3.6 %copy-start.10 = (s32[8]{0:T(128)S(1)}, s32[8]{0:T(128)}, u32[]{:S(2)}) copy-start(s32[8]{0:T(128)} %count_middle.1) | copy-start | bytes 100
  22.8 3.6 %copy-start.11 = (s32[4]{0:T(128)S(1)}, s32[4]{0:T(128)}, u32[]{:S(2)}) copy-start(s32[4]{0:T(128)} %count_top.1) | copy-start | bytes 52
